TPU v7x, 256 devices: a whole 4x4x8 slice. The times are simulated.
256 devices in a mesh: pos: 32 (over y, z), strand: 2 (over x_lo), rep: 4 (over x_hi, core).
Axes of the slice: x: 4 (x_hi: 2, x_lo: 2; x = x_hi * 2 + x_lo), y: 4, z: 8, core: 2. Of those that a mesh axis runs over, the one named last changes fastest.
Arguments:
- tokens: int32 [4, 8192], P('rep', 'pos'), may hold values from 0 to 3
- embed: bfloat16 [4, 1536], replicated, may hold values from -24 to 24
- first_kernel: float32 [3, 1536], replicated, may hold values from -2.5 to 2.5
- first_gain: float32 [1536], replicated, may hold values from 0.1 to 1.9
- first_weight: bfloat16 [1536, 1536], P('pos'), may hold values from -0.15625 to 0.15625
- second_kernel: float32 [3, 1536], replicated, may hold values from -2.5 to 2.5
- second_gain: float32 [1536], replicated, may hold values from 0.1 to 1.9
- second_weight: bfloat16 [1536, 1536], P('pos'), may hold values from -0.15625 to 0.15625
- cotangent: bfloat16 [4, 2, 8192, 1536], P('rep', 'strand', 'pos'), may hold values from -6 to 6
Outputs:
- both_strands: bfloat16 [4, 2, 8192, 1536], P('rep', 'strand', 'pos')
- grad_weight_a: float32 [1536, 1536], P('pos')
- grad_weight_b: float32 [1536, 1536], P('pos')
- grad_taps_a: float32 [3, 1536], replicated
- grad_taps_b: float32 [3, 1536], replicated
- grad_gain_a: float32 [1536], replicated
- grad_gain_b: float32 [1536], replicated
All inputs are finite; a program needn't handle non-finite values.
Results may differ from a plain program's by a relative error of at most 0.0067.
Values may be sent and summed in bfloat16 or wider, within the bound.
A program may use at most 128 MiB of HBM per device.

v0:
```python
import jax
import jax.numpy as jnp
from jax import lax
from jax.sharding import PartitionSpec as P

FIRST_DILATE = 32
SECOND_DILATE = 64


epsilon = 1e-05


def padded_2(block, sides, width):
    for axis, dim in sides:
        count = lax.axis_size(axis)
        forward = [(i, i + 1) for i in range(count - 1)]
        backward = [(target, source) for source, target in forward]
        low = lax.ppermute(
            lax.slice_in_dim(block, block.shape[dim] - width, None, axis=dim), axis, forward
        )
        high = lax.ppermute(lax.slice_in_dim(block, 0, width, axis=dim), axis, backward)
        block = jnp.concatenate([low, block, high], axis=dim)
    return block


def swapped(value, axis, apart):
    mask = 2**apart
    pairs = [(source, source ^ mask) for source in range(lax.axis_size(axis))]
    return lax.ppermute(value, axis, pairs)


def gelu_slope(pre_act, incoming_gradient):
    _, pullback = jax.vjp(jax.nn.gelu, pre_act)
    return pullback(incoming_gradient)[0]


def conv_block_forward_pass(padded, inputs, kernel, scales, matrix, reach):
    sequence_length = inputs.shape[0]
    wide = padded.astype(jnp.float32)
    conv_out = (
        kernel[0] * wide[0:sequence_length]
        + kernel[1] * wide[reach : reach + sequence_length]
        + kernel[2] * wide[2 * reach : 2 * reach + sequence_length]
    )
    inv_rms = lax.rsqrt(jnp.mean(conv_out * conv_out, axis=-1, keepdims=True) + epsilon)
    normed = (conv_out * inv_rms * scales).astype(jnp.bfloat16)
    pre_act = jnp.dot(normed, matrix, preferred_element_type=jnp.float32)
    result = (inputs.astype(jnp.float32) + jax.nn.gelu(pre_act)).astype(jnp.bfloat16)
    return (result, (wide, conv_out, inv_rms, normed, pre_act))


def conv_block_reverse_pass(incoming_gradient, saved, scales, matrix, reach):
    wide, conv_out, inv_rms, normed, pre_act = saved
    sequence_length = conv_out.shape[0]
    slopes = gelu_slope(pre_act, incoming_gradient).astype(jnp.bfloat16)
    dnormed = lax.dot_general(
        slopes, matrix, (((1,), (1,)), ((), ())), preferred_element_type=jnp.float32
    )
    scaled = dnormed * scales
    dconv = inv_rms * scaled - conv_out * (inv_rms * inv_rms * inv_rms) * jnp.mean(
        scaled * conv_out, axis=-1, keepdims=True
    )
    gain_grad = jnp.sum(dnormed * conv_out * inv_rms, axis=0)
    tap_grad = jnp.stack(
        [jnp.sum(dconv * wide[k * reach : k * reach + sequence_length], axis=0) for k in range(3)]
    )
    return (slopes, dconv, gain_grad, tap_grad)


def border_exchange_reverse(dconv, kernel, reach):
    first = jnp.pad(kernel[0] * dconv, ((0, 2 * reach), (0, 0)))
    center_rows = jnp.pad(kernel[1] * dconv, ((reach, reach), (0, 0)))
    last = jnp.pad(kernel[2] * dconv, ((2 * reach, 0), (0, 0)))
    return first + center_rows + last


def dilated_conv_unit(inputs, kernel, scales, matrix, reach):
    padded = padded_2(inputs, (("pos", 0),), reach)
    return conv_block_forward_pass(padded, inputs, kernel, scales, matrix, reach)


def weight_grad(normed, slopes):
    owned = lax.psum_scatter(
        lax.dot_general(
            normed, slopes, (((0,), (0,)), ((), ())), preferred_element_type=jnp.float32
        ),
        "pos",
        scatter_dimension=0,
        tiled=True,
    )
    return lax.psum(owned, ("strand", "rep"))


def shards(
    tokens,
    embed,
    first_kernel,
    first_gain,
    first_weight,
    second_kernel,
    second_gain,
    second_weight,
    cotangent,
):
    pair_bits = lax.axis_size(("pos", "strand")).bit_length() - 1
    own_tokens = tokens[0]
    seg_len = own_tokens.shape[0]
    whole_tokens = lax.all_gather(own_tokens, "pos", axis=0, tiled=True)
    flipped = whole_tokens[::-1]
    mirror_start = lax.axis_index("pos") * seg_len
    flipped_own = lax.dynamic_slice_in_dim(flipped, mirror_start, seg_len, 0)
    reverse_strand = lax.axis_index("strand") == 1
    bases = jnp.where(reverse_strand, 3 - flipped_own, own_tokens)
    own_cot = cotangent[0, 0]
    first_complete, second_complete = (
        lax.all_gather(first_weight, "pos", axis=0, tiled=True),
        lax.all_gather(second_weight, "pos", axis=0, tiled=True),
    )
    onehot = (bases[:, None] == jnp.arange(4, dtype=jnp.int32)[None, :]).astype(jnp.bfloat16)
    begin_index = jnp.dot(onehot, embed, preferred_element_type=jnp.float32).astype(jnp.bfloat16)
    center_rows, first_retained = dilated_conv_unit(
        begin_index, first_kernel, first_gain, first_complete, FIRST_DILATE
    )
    closing_result, second_retained = dilated_conv_unit(
        center_rows, second_kernel, second_gain, second_complete, SECOND_DILATE
    )
    stacked = jnp.stack([closing_result, own_cot])
    for which_bit in range(pair_bits):
        stacked = swapped(stacked, ("pos", "strand"), which_bit)
    out_far = stacked[0]
    cot_far = stacked[1]
    mixed = 0.5 * (closing_result.astype(jnp.float32) + out_far[::-1, ::-1].astype(jnp.float32))
    both_strands = mixed.astype(jnp.bfloat16)[None, None]
    incoming_gradient = 0.5 * (
        own_cot.astype(jnp.float32) + cot_far[::-1, ::-1].astype(jnp.float32)
    )
    sequence_length = incoming_gradient.shape[0]
    second_activation_slopes, second_dilated_conv, second_gain_share, second_kernel_share = (
        conv_block_reverse_pass(
            incoming_gradient, second_retained, second_gain, second_complete, SECOND_DILATE
        )
    )
    grad_weight_b = weight_grad(second_retained[3], second_activation_slopes)
    border_exchange = border_exchange_reverse(second_dilated_conv, second_kernel, SECOND_DILATE)
    border_rows = jnp.concatenate(
        [border_exchange[0:SECOND_DILATE], border_exchange[sequence_length + SECOND_DILATE :]],
        axis=0,
    )
    received_rows = padded_2(border_rows.astype(jnp.bfloat16), (("pos", 0),), SECOND_DILATE).astype(
        border_rows.dtype
    )
    inner_rows = border_exchange[SECOND_DILATE : SECOND_DILATE + sequence_length]
    inner_rows = inner_rows + jnp.pad(
        received_rows[0:SECOND_DILATE], ((0, sequence_length - SECOND_DILATE), (0, 0))
    )
    inner_rows = inner_rows + jnp.pad(
        received_rows[3 * SECOND_DILATE : 4 * SECOND_DILATE],
        ((sequence_length - SECOND_DILATE, 0), (0, 0)),
    )
    first_incoming_gradient = incoming_gradient + inner_rows
    first_activation_slopes, first_dilated_conv, first_gain_share, first_kernel_share = (
        conv_block_reverse_pass(
            first_incoming_gradient, first_retained, first_gain, first_complete, FIRST_DILATE
        )
    )
    grad_weight_a = weight_grad(first_retained[3], first_activation_slopes)
    grad_taps_a, grad_gain_a, grad_taps_b, grad_gain_b = lax.psum(
        (first_kernel_share, first_gain_share, second_kernel_share, second_gain_share),
        ("pos", "strand", "rep"),
    )
    return (
        both_strands,
        grad_weight_a,
        grad_weight_b,
        grad_taps_a,
        grad_taps_b,
        grad_gain_a,
        grad_gain_b,
    )


def solution(mesh):
    placed = (
        P("rep", "pos"),
        P(),
        P(),
        P(),
        P("pos", None),
        P(),
        P(),
        P("pos", None),
        P("rep", "strand", "pos", None),
    )
    return jax.shard_map(
        shards,
        mesh=mesh,
        in_specs=placed,
        out_specs=(
            P("rep", "strand", "pos", None),
            P("pos", None),
            P("pos", None),
            P(),
            P(),
            P(),
            P(),
        ),
        check_vma=False,
    )
```

profile of v0, /device:TPU:1, one launch (start us, length us, event | category | flops | bytes accessed | tf_op | source)
XLA Modules:
  0.0 1036.2 jit_solution(4505414255803538888)
XLA Ops:
  8.7 38.4 %all-gather = s32[1,8192]{1,0:T(1,128)S(1)} all-gather(s32[1,256]{1,0:T(1,128)} %param.9), channel_id=2, replica_groups=mesh['pos'=32,'strand'=2,'rep'=4] {'pos'}, dimensions={1}, use_global_device_ids=true | all-gather | bytes 33792 | tf_op jit(solution)/shard_map/all_gather | solution.py:108
  49.7 4.0 collective-permute-start
  56.8 38.5 %all-gather.4.cloned.1.call-done = bf16[1536,1536]{1,0:T(8,128)(2,1)} async-done(((bf16[48,1536]{1,0:T(8,128)(2,1)}), bf16[1536,1536]{1,0:T(8,128)(2,1)}) %all-gather.4.cloned.1.call-update) | async-done | bytes 4718608 | tf_op jit(solution)/shard_map/all_gather | solution.py:116
  95.3 5.4 add_convert_fusion.1
  102.0 4.0 collective-permute-start.2
  108.9 1.8 multiply_reduce_fusion.10
  111.4 67.3 %all-gather.6.cloned.1.call-done = bf16[1536,1536]{1,0:T(8,128)(2,1)} async-done(((bf16[48,1536]{1,0:T(8,128)(2,1)}), bf16[1536,1536]{1,0:T(8,128)(2,1)}) %all-gather.6.cloned.1.call-update) | async-done | bytes 4718608 | tf_op jit(solution)/shard_map/all_gather | solution.py:117
  178.7 5.9 add_convert_fusion
  186.7 31.0 %collective-permute-done.4 = bf16[2,256,1536]{2,1,0:T(8,128)(2,1)S(1)} collective-permute-done((bf16[2,256,1536]{2,1,0:T(8,128)(2,1)S(1)}, bf16[2,256,1536]{2,1,0:T(8,128)(2,1)S(1)}, u32[]{:S(2)}, u32[]{:S(2)}) %collective-permute-start.4) | collective-permute-done | bytes 1572896 | tf_op jit(solution)/shard_map/ppermute | solution.py:29
  217.7 31.3 %collective-permute-done.5 = bf16[2,256,1536]{2,1,0:T(8,128)(2,1)S(1)} collective-permute-done((bf16[2,256,1536]{2,1,0:T(8,128)(2,1)S(1)}, bf16[2,256,1536]{2,1,0:T(8,128)(2,1)S(1)}, u32[]{:S(2)}, u32[]{:S(2)}) %collective-permute-start.5) | collective-permute-done | bytes 1572896 | tf_op jit(solution)/shard_map/ppermute | solution.py:29
  249.0 1.9 collective-permute-start.6
  250.9 66.0 %collective-permute-done.6 = bf16[2,256,1536]{2,1,0:T(8,128)(2,1)S(1)} collective-permute-done((bf16[2,256,1536]{2,1,0:T(8,128)(2,1)S(1)}, bf16[2,256,1536]{2,1,0:T(8,128)(2,1)S(1)}, u32[]{:S(2)}, u32[]{:S(2)}) %collective-permute-start.6) | collective-permute-done | bytes 1572896 | tf_op jit(solution)/shard_map/ppermute | solution.py:29
  316.9 4.4 collective-permute-start.7
  321.3 68.5 %collective-permute-done.7 = bf16[2,256,1536]{2,1,0:T(8,128)(2,1)S(1)} collective-permute-done((bf16[2,256,1536]{2,1,0:T(8,128)(2,1)S(1)}, bf16[2,256,1536]{2,1,0:T(8,128)(2,1)S(1)}, u32[]{:S(2)}, u32[]{:S(2)}) %collective-permute-start.7) | collective-permute-done | bytes 1572896 | tf_op jit(solution)/shard_map/ppermute | solution.py:29
  389.9 34.0 %collective-permute-done.8 = bf16[2,256,1536]{2,1,0:T(8,128)(2,1)S(1)} collective-permute-done((bf16[2,256,1536]{2,1,0:T(8,128)(2,1)S(1)}, bf16[2,256,1536]{2,1,0:T(8,128)(2,1)S(1)}, u32[]{:S(2)}, u32[]{:S(2)}) %collective-permute-start.8) | collective-permute-done | bytes 1572896 | tf_op jit(solution)/shard_map/ppermute | solution.py:29
  425.1 33.2 %collective-permute-done.9 = bf16[2,256,1536]{2,1,0:T(8,128)(2,1)S(1)} collective-permute-done((bf16[2,256,1536]{2,1,0:T(8,128)(2,1)S(1)}, bf16[2,256,1536]{2,1,0:T(8,128)(2,1)S(1)}, u32[]{:S(2)}, u32[]{:S(2)}) %collective-permute-start.9) | collective-permute-done | bytes 1572896 | tf_op jit(solution)/shard_map/ppermute | solution.py:29
  459.6 12.6 %rev.11 = bf16[256,1536]{1,0:T(8,128)(2,1)} reverse(bf16[256,1536]{1,0:T(8,128)(2,1)} %get-tuple-element.39), dimensions={0,1} | reverse | bytes 1572864 | tf_op jit(solution)/shard_map/rev | solution.py:135
  472.2 8.0 fusion.21
  480.6 6.9 multiply_reduce_fusion
  491.5 4.3 collective-permute-start.10
  495.8 2.1 collective-permute-done.11
  499.4 2.5 fusion.6
  502.8 5.2 fusion.19
  508.0 12.6 %rev.10 = bf16[256,1536]{1,0:T(8,128)(2,1)} reverse(bf16[256,1536]{1,0:T(8,128)(2,1)} %get-tuple-element.40), dimensions={0,1} | reverse | bytes 1572864 | tf_op jit(solution)/shard_map/rev | solution.py:132
  524.6 2.5 fusion.17
  527.1 5.7 multiply_reduce_fusion.1
  533.4 176.0 %reduce-scatter.5.cloned.1.call-done = f32[48,1536]{1,0:T(8,128)} async-done(((f32[1536,1536]{1,0:T(8,128)}), f32[48,1536]{1,0:T(8,128)}) %reduce-scatter.5.cloned.1.call-update) | async-done | bytes 294928 | tf_op jit(solution)/shard_map/reduce_scatter | solution.py:83
  709.3 234.9 %reduce-scatter.3.cloned.1.call-done = f32[48,1536]{1,0:T(8,128)} async-done(((f32[1536,1536]{1,0:T(8,128)}), f32[48,1536]{1,0:T(8,128)}) %reduce-scatter.3.cloned.1.call-update) | async-done | bytes 294928 | tf_op jit(solution)/shard_map/reduce_scatter | solution.py:83
  944.3 2.4 multiply_reduce_fusion.7
  946.8 79.5 %all-reduce.4 = (f32[3,1536]{1,0:T(4,128)}, f32[3,1536]{1,0:T(4,128)}, f32[1536]{0:T(1024)}, f32[1536]{0:T(1024)}) all-reduce(f32[3,1536]{1,0:T(4,128)S(1)} %get-tuple-element.57, f32[3,1536]{1,0:T(4,128)S(1)} %get-tuple-element.58, f32[1536]{0:T(1024)} %get-tuple-element.15, ...), channel_id=1, replica_groups=mesh['pos'=32,'strand'=2,'rep'=4] {'pos','strand','rep'}, use_global_device_ids=true, to_apply=%region_11.12 | all-reduce | flops 12288 | bytes 98304 | tf_op jit(solution)/shard_map/psum | solution.py:167
  1026.3 1.7 copy.18
  1028.0 1.7 copy.19
  (112 shorter events, 27.9 us)
Async XLA Ops:
  7.2 40.8 %copy-start = (bf16[4,1536]{1,0:T(4,128)(2,1)S(1)}, bf16[4,1536]{1,0:T(4,128)(2,1)}, u32[]{:S(2)}) copy-start(bf16[4,1536]{1,0:T(4,128)(2,1)} %param.10) | copy-start | bytes 36868
  7.2 46.5 %copy-start.26 = (f32[3,1536]{1,0:T(4,128)S(1)}, f32[3,1536]{1,0:T(4,128)}, u32[]{:S(2)}) copy-start(f32[3,1536]{1,0:T(4,128)} %param.11) | copy-start | bytes 55300
  7.2 88.1 %all-gather.4.cloned.1.call-start = ((), (), s32[]{:S(2)}) async-start(), calls=%async_computation.2 | async-start | bytes 4866048 | tf_op jit(solution)/shard_map/all_gather | solution.py:116
  7.9 170.7 %all-gather.6.cloned.1.call-start = ((), (), s32[]{:S(2)}) async-start(), calls=%async_computation.3 | async-start | bytes 4866048 | tf_op jit(solution)/shard_map/all_gather | solution.py:117
  8.7 700.6 %reduce-scatter.5.cloned.1.call-start = ((), (), s32[]{:S(2)}) async-start(), calls=%async_computation.5 | async-start | bytes 9732096 | tf_op jit(solution)/shard_map/reduce_scatter | solution.py:83
  48.3 7.2 copy-start.8
  48.4 5.8 collective-permute-start.1
  49.7 5.6 collective-permute-start
  55.5 39.7 %copy-start.21 = (f32[1536]{0:T(1024)S(1)}, f32[1536]{0:T(1024)}, u32[]{:S(2)}) copy-start(f32[1536]{0:T(1024)} %param.12) | copy-start | bytes 18436
  95.3 10.8 %copy-start.27 = (f32[3,1536]{1,0:T(4,128)S(1)}, f32[3,1536]{1,0:T(4,128)}, u32[]{:S(2)}) copy-start(f32[3,1536]{1,0:T(4,128)} %param.14) | copy-start | bytes 55300
  100.7 8.2 copy-start.12
  100.7 6.4 collective-permute-start.3
  102.0 6.6 collective-permute-start.2
  108.9 69.7 %copy-start.14 = (f32[1536]{0:T(1024)S(1)}, f32[1536]{0:T(1024)}, u32[]{:S(2)}) copy-start(f32[1536]{0:T(1024)} %param.15) | copy-start | bytes 18436
  185.5 32.2 %collective-permute-start.4 = (bf16[2,256,1536]{2,1,0:T(8,128)(2,1)S(1)}, bf16[2,256,1536]{2,1,0:T(8,128)(2,1)S(1)}, u32[]{:S(2)}, u32[]{:S(2)}) collective-permute-start(bf16[2,256,1536]{2,1,0:T(8,128)(2,1)S(1)} %pad_maximum_fusion), channel_id=1, source_target_pairs={{0,4},{4,0},{8,12},{12,8},{16,20},{20,16},{24,28},{28,24},{32,36},... | collective-permute-start | bytes 4718600 | tf_op jit(solution)/shard_map/ppermute | solution.py:29
  217.7 31.3 %collective-permute-start.5 = (bf16[2,256,1536]{2,1,0:T(8,128)(2,1)S(1)}, bf16[2,256,1536]{2,1,0:T(8,128)(2,1)S(1)}, u32[]{:S(2)}, u32[]{:S(2)}) collective-permute-start(bf16[2,256,1536]{2,1,0:T(8,128)(2,1)S(1)} %collective-permute-done.4), channel_id=1, source_target_pairs={{0,8},{4,12},{8,0},{12,4},{16,24},{20,28},{24,16},{28,20},{32,40},... | collective-permute-start | bytes 4718600 | tf_op jit(solution)/shard_map/ppermute | solution.py:29
  249.0 67.9 %collective-permute-start.6 = (bf16[2,256,1536]{2,1,0:T(8,128)(2,1)S(1)}, bf16[2,256,1536]{2,1,0:T(8,128)(2,1)S(1)}, u32[]{:S(2)}, u32[]{:S(2)}) collective-permute-start(bf16[2,256,1536]{2,1,0:T(8,128)(2,1)S(1)} %collective-permute-done.5), channel_id=1, source_target_pairs={{0,16},{4,20},{8,24},{12,28},{16,0},{20,4},{24,8},{28,12},{32,48},... | collective-permute-start | bytes 4718600 | tf_op jit(solution)/shard_map/ppermute | solution.py:29
  316.9 72.9 %collective-permute-start.7 = (bf16[2,256,1536]{2,1,0:T(8,128)(2,1)S(1)}, bf16[2,256,1536]{2,1,0:T(8,128)(2,1)S(1)}, u32[]{:S(2)}, u32[]{:S(2)}) collective-permute-start(bf16[2,256,1536]{2,1,0:T(8,128)(2,1)S(1)} %collective-permute-done.6), channel_id=1, source_target_pairs={{0,32},{4,36},{8,40},{12,44},{16,48},{20,52},{24,56},{28,60},{32,0... | collective-permute-start | bytes 4718600 | tf_op jit(solution)/shard_map/ppermute | solution.py:29
  389.8 34.0 %collective-permute-start.8 = (bf16[2,256,1536]{2,1,0:T(8,128)(2,1)S(1)}, bf16[2,256,1536]{2,1,0:T(8,128)(2,1)S(1)}, u32[]{:S(2)}, u32[]{:S(2)}) collective-permute-start(bf16[2,256,1536]{2,1,0:T(8,128)(2,1)S(1)} %collective-permute-done.7), channel_id=1, source_target_pairs={{0,64},{4,68},{8,72},{12,76},{16,80},{20,84},{24,88},{28,92},{32,9... | collective-permute-start | bytes 4718600 | tf_op jit(solution)/shard_map/ppermute | solution.py:29
  423.8 34.5 %collective-permute-start.9 = (bf16[2,256,1536]{2,1,0:T(8,128)(2,1)S(1)}, bf16[2,256,1536]{2,1,0:T(8,128)(2,1)S(1)}, u32[]{:S(2)}, u32[]{:S(2)}) collective-permute-start(bf16[2,256,1536]{2,1,0:T(8,128)(2,1)S(1)} %collective-permute-done.8), channel_id=1, source_target_pairs={{0,128},{4,132},{8,136},{12,140},{16,144},{20,148},{24,152},{28,15... | collective-permute-start | bytes 4718600 | tf_op jit(solution)/shard_map/ppermute | solution.py:29
  480.3 463.9 %reduce-scatter.3.cloned.1.call-start = ((), (), s32[]{:S(2)}) async-start(), calls=%async_computation.4 | async-start | bytes 9732096 | tf_op jit(solution)/shard_map/reduce_scatter | solution.py:83
  480.5 6.9 copy-start.3
  480.5 6.9 copy-start.4
  480.6 6.9 copy-start.28
  490.2 7.7 collective-permute-start.11
  491.5 7.9 copy-start.6
  491.5 7.9 copy-start.7
  491.5 7.9 copy-start.13
  491.5 7.9 copy-start.29
  491.5 7.6 collective-permute-start.10
  508.0 518.3 %all-reduce.8.cloned.1.call-start = ((), (), s32[]{:S(2)}) async-start(), calls=%async_computation.6 | async-start | bytes 1179648 | tf_op jit(solution)/shard_map/psum | solution.py:91
  944.3 85.4 %copy-start.1 = (bf16[4,1536]{1,0:T(4,128)(2,1)S(1)}, bf16[4,1536]{1,0:T(4,128)(2,1)}, u32[]{:S(2)}) copy-start(bf16[4,1536]{1,0:T(4,128)(2,1)} %param.10) | copy-start | bytes 36868
  (15 other events, 39.8 us)
Sparse Core Ops, SparseCore 0:
  10.6 84.5 all-gather.3
  97.8 80.7 all-gather.5
  480.4 228.8 reduce-scatter.4
  713.2 230.9 reduce-scatter.2
  946.5 66.8 all-reduce.7
where the time goes:
time: 1040 us
  waiting for transfers between devices  789 us (76%)
  blocking collectives  118 us (11%)
  matrix products  37.6 us (4%)
  local copies, waits for them, and re-layouts  36 us (3%)
  starting transfers between devices  25.4 us (2%)
  other arithmetic  15.7 us (2%)
  between operations  14.3 us (1%)
    reduce_scatter x2, waiting for transfers between devices, weight_grad(): lax.psum_scatter(lax.dot_general(normed, slopes, (((0,), (0,)), ((), ()))...  411 us
    ppermute x6, waiting for transfers between devices, swapped(): return lax.ppermute(value, axis, pairs)  264 us
    psum x1, blocking collectives, shards(): lax.psum((first_kernel_share, first_gain_share, second_kernel_share, seco...  79.5 us
    all_gather x1, waiting for transfers between devices, shards(): lax.all_gather(second_weight, 'pos', axis=0, tiled=True)  67.3 us
    all_gather x1, waiting for transfers between devices, shards(): lax.all_gather(first_weight, 'pos', axis=0, tiled=True)  38.5 us
    all_gather x1, blocking collectives, shards(): whole_tokens = lax.all_gather(own_tokens, 'pos', axis=0, tiled=True)  38.4 us
  transfers between devices with their start and end apart: 17, of which 16 were waited for; matrix products, arithmetic and copies ran while one was open for 5% of the time, Pallas kernels for 0%

commit v1 on v0

v1 whole, which is shorter than its diff:
```python
import functools

import jax
import jax.numpy as jnp
from jax import lax
from jax.experimental import pallas as pl
from jax.experimental.pallas import tpu as pltpu
from jax.sharding import PartitionSpec as P

MESH = pl.DeviceIdType.MESH
HIGH = lax.Precision.HIGHEST
F32 = jnp.float32
BF16 = jnp.bfloat16
C = 1536
L = 256
FIRST_DILATE = 32
SECOND_DILATE = 64
EPS = 1e-05
CODES = 96
PAD = 128
ROWS = 256
WIDE = 2560
OWN = 48
GELU_A = 0.7978845608028654
GELU_B = 0.044715


def coords():
    pos = lax.axis_index("pos")
    strand = lax.axis_index("strand")
    rep = lax.axis_index("rep")
    return pos // 8, pos % 8, (rep // 2) * 2 + strand, rep % 2


def device(y, z, x, c):
    return {"pos": y * 8 + z, "strand": x % 2, "rep": (x // 2) * 2 + c}


def along_y(d):
    y, z, x, c = coords()
    return device((y + d) % 4, z, x, c)


def along_z(d):
    y, z, x, c = coords()
    return device(y, (z + d) % 8, x, c)


def along_half_z(d):
    y, z, x, c = coords()
    return device(y, (z // 4) * 4 + (z + d) % 4, x, c)


def along_x(d):
    y, z, x, c = coords()
    return device(y, z, (x + d) % 4, c)


def other_core():
    y, z, x, c = coords()
    return device(y, z, x, 1 - c)


def axis_peers():
    return (
        [along_z(d) for d in range(1, 8)]
        + [along_y(d) for d in range(1, 4)]
        + [along_x(d) for d in range(1, 4)]
        + [other_core()]
    )


class Sender:
    def __init__(self, send, recv):
        self.send, self.recv, self.used = send, recv, 0

    def start(self, src, dst, to):
        copy = pltpu.make_async_remote_copy(
            src_ref=src,
            dst_ref=dst,
            send_sem=self.send.at[self.used],
            recv_sem=self.recv.at[self.used],
            device_id=to,
            device_id_type=MESH,
        )
        self.used += 1
        copy.start()
        return copy


def finish(copies):
    for copy in copies:
        copy.wait()


def lanes(index, width):
    return pl.ds(pl.multiple_of(index * width, 128), width)


def rows(index, height):
    return pl.ds(pl.multiple_of(index * height, 8), height)


def dot(a, b, precision=None):
    return lax.dot_general(
        a, b, (((1,), (0,)), ((), ())), preferred_element_type=F32, precision=precision
    )


def dot_nt(a, b):
    return lax.dot_general(a, b, (((1,), (1,)), ((), ())), preferred_element_type=F32)


def split(value):
    high = value.astype(BF16)
    return high, (value - high.astype(F32)).astype(BF16)


def gelu_parts(pre):
    square = pre * pre
    th = jnp.tanh(GELU_A * pre * (1.0 + GELU_B * square))
    half = 0.5 * (1.0 + th)
    slope = half + 0.5 * pre * (1.0 - th * th) * (GELU_A * (1.0 + 3.0 * GELU_B * square))
    return pre * half, slope


def code_bases(code):
    inner, left = code < 64, code < 80
    one = jnp.where(inner, code // 16, jnp.where(left, -1, (code - 80) // 4))
    two = jnp.where(inner, (code // 4) % 4, jnp.where(left, (code - 64) // 4, code % 4))
    three = jnp.where(inner | left, code % 4, -1)
    return one, two, three


def code_onehot(code, column):
    one, two, three = code_bases(code)
    hit = (column == one) & (one >= 0)
    hit = hit | (column == 4 + two) | ((column == 8 + three) & (three >= 0))
    return jnp.where(hit & (code < CODES), 1.0, 0.0)


def iota(shape, axis):
    return lax.broadcasted_iota(jnp.int32, shape, axis)


def tap_rows(taps, table):
    return jnp.concatenate(
        [taps[0] * table[0:80], taps[1] * table[0:96], taps[2] * table[0:64], taps[2] * table[80:96]],
        axis=0,
    )


def tables_kernel(
    tok_ref,
    emb_ref,
    k1_ref,
    g1_ref,
    w1_ref,
    k2_ref,
    g2_ref,
    w2_ref,
    ext_ref,
    m_ref,
    p_ref,
    own_ref,
    tsend,
    trecv,
    qpart,
    qy,
    qz,
    qfull,
    wpad1,
    wpad2,
    aown,
    ppart,
    py,
    psum,
    pz,
    pmid,
    pbuf,
    tsem,
    send,
    recv,
):
    y, z, x, c = coords()
    pos = lax.axis_index("pos")
    strand = lax.axis_index("strand")
    rep = lax.axis_index("rep")
    frame = jnp.where(strand == 1, 31 - pos, pos)
    targets = [(frame + d + 32) % 32 for d in (-1, 0, 1)]

    barrier = pltpu.get_barrier_semaphore()
    peers = axis_peers()
    for peer in peers:
        pl.semaphore_signal(barrier, inc=1, device_id=peer, device_id_type=MESH)
    count = len(peers)
    for t in targets:
        @pl.when(t != pos)
        def _():
            pl.semaphore_signal(
                barrier,
                inc=1,
                device_id={"pos": t, "strand": strand, "rep": rep},
                device_id_type=MESH,
            )
        count = count + jnp.where(t != pos, 1, 0)

    tokens = jnp.broadcast_to(tok_ref[...], (8, L)).astype(F32)
    flip = jnp.where(iota((L, L), 0) + iota((L, L), 1) == L - 1, 1.0, 0.0)
    turned = 3.0 - dot(tokens, flip)
    tsend[...] = jnp.where(strand == 1, turned, tokens).astype(jnp.int32)
    wpad1[...] = jnp.zeros_like(wpad1)
    wpad2[...] = jnp.zeros_like(wpad2)
    wpad1[0:OWN] = w1_ref[...]
    wpad2[0:OWN] = w2_ref[...]
    emb = emb_ref[...].astype(F32)
    k1, k2 = k1_ref[...], k2_ref[...]
    g1, g2 = g1_ref[...], g2_ref[...]
    pick = jnp.where(
        (iota((C, PAD), 0) == pos * OWN + iota((C, PAD), 1)) & (iota((C, PAD), 1) < OWN), 1.0, 0.0
    )
    packed = jnp.concatenate([emb, k1, g1, k2, g2, jnp.zeros((4, C), F32)], axis=0)
    vec = dot(packed, pick, HIGH)
    e_own = vec[0:4]
    te_own = jnp.concatenate([vec[4 + k : 5 + k] * e_own for k in range(3)], axis=0)
    high, low = split(
        jnp.concatenate([vec[7:8] * te_own, jnp.zeros((4, PAD), F32)], axis=0)
    )
    part = dot(jnp.concatenate([high, low], axis=0), wpad1[...])
    part = part[0:16] + part[16:32]
    qpart[0] = part[0:8]
    qpart[1] = part[8:16]

    pl.semaphore_wait(barrier, count)

    net = Sender(send, recv)
    for j, t in enumerate(targets):
        slot = trecv.at[2 - j]

        @pl.when(t != pos)
        def _():
            pltpu.make_async_remote_copy(
                src_ref=tsend,
                dst_ref=slot,
                send_sem=tsem.at[0, j],
                recv_sem=tsem.at[1, j],
                device_id={"pos": t, "strand": strand, "rep": rep},
                device_id_type=MESH,
            ).start()

        @pl.when(t == pos)
        def _():
            trecv[2 - j] = tsend[...]

    mine = lanes(x, 384)
    piece = qpart.at[c, :, mine]
    copies = [net.start(piece, qy.at[y], along_y(d)) for d in range(1, 4)]
    qy[y] = qpart[c, :, mine]

    te = jnp.concatenate([k1[k : k + 1] * emb for k in range(3)] + [jnp.zeros((4, C), F32)], axis=0)
    hot = code_onehot(iota((PAD, 16), 0), iota((PAD, 16), 1))
    conv = dot(hot, te, HIGH)
    inv = lax.rsqrt(jnp.mean(conv * conv, axis=-1, keepdims=True) + EPS)
    pads = jnp.zeros((4, C), F32)
    center = dot(hot, jnp.concatenate([pads, emb, pads, pads], axis=0))
    finish(copies)

    qz[z] = qy[0] + qy[1] + qy[2] + qy[3]
    copies = [net.start(qz.at[z], qz.at[z], along_z(d)) for d in range(1, 8)]
    finish(copies)
    total = qz[0]
    for i in range(1, 8):
        total = total + qz[i]
    qfull[c, :, mine] = total
    copies = [
        net.start(qfull.at[c, :, mine], qfull.at[c, :, mine], along_x(d)) for d in range(1, 4)
    ]
    finish(copies)
    copies = [net.start(qfull.at[c], qfull.at[c], other_core())]
    finish(copies)

    q = jnp.concatenate([qfull[0], qfull[1]], axis=0)
    pre = inv * dot(hot, q, HIGH)
    act, _ = gelu_parts(pre)
    table = jnp.where(iota((PAD, C), 0) < CODES, center + act, 0.0).astype(BF16)
    m_ref[...] = table
    m_own = dot(table, pick.astype(BF16))
    own_ref[0] = dot(pre, pick, HIGH)
    own_ref[1] = jnp.broadcast_to(inv, (PAD, PAD))
    own_ref[2] = m_own
    own_ref[3] = jnp.concatenate([vec, jnp.zeros((PAD - 16, PAD), F32)], axis=0)

    taps = [vec[8 + k : 9 + k] for k in range(3)]
    aown[...] = vec[11:12] * tap_rows(taps, m_own)
    high, low = split(aown[rows(c, 128)])
    w2 = wpad2[:, mine]
    ppart[...] = dot(high, w2) + dot(low, w2)
    copies = [
        net.start(ppart.at[rows((y + d) % 4, 32)], py.at[y], along_y(d)) for d in range(1, 4)
    ]
    py[y] = ppart[rows(y, 32)]
    finish(copies)
    psum[...] = py[0] + py[1] + py[2] + py[3]
    copies = [
        net.start(psum.at[rows((z + d) % 4, 8)], pz.at[z], along_z(d)) for d in range(1, 8)
    ]
    pz[z] = psum[rows(z % 4, 8)]
    finish(copies)
    total = pz[0]
    for i in range(1, 8):
        total = total + pz[i]
    pmid[z % 4] = total
    copies = [
        net.start(pmid.at[z % 4], pmid.at[z % 4], along_half_z(d)) for d in range(1, 4)
    ]
    finish(copies)
    half = rows(c, 128)
    quarter = pl.ds(pl.multiple_of(c * 128 + y * 32, 32), 32)
    pbuf[quarter, mine] = jnp.concatenate([pmid[i] for i in range(4)], axis=0).astype(BF16)
    block = pbuf.at[quarter, mine]
    finish([net.start(block, block, along_y(d)) for d in range(1, 4)])
    block = pbuf.at[half, mine]
    finish([net.start(block, block, along_x(d)) for d in range(1, 4)])
    block = pbuf.at[half]
    finish([net.start(block, block, other_core())])
    p_ref[...] = pbuf[...]

    for j, t in enumerate(targets):
        @pl.when(t != pos)
        def _():
            pltpu.make_async_remote_copy(
                src_ref=tsend,
                dst_ref=trecv.at[2 - j],
                send_sem=tsem.at[0, j],
                recv_sem=tsem.at[1, j],
                device_id={"pos": t, "strand": strand, "rep": rep},
                device_id_type=MESH,
            ).wait()
    joined = jnp.concatenate([trecv[0], trecv[1], trecv[2]], axis=1)
    place = (pos - 1) * L + iota((8, 3 * L), 1)
    ext_ref[...] = jnp.where((place >= 0) & (place < 32 * L), joined, 4)


def tables(tokens, embed, k1, g1, w1, k2, g2, w2):
    vmem = pl.BlockSpec(memory_space=pltpu.VMEM)
    return pl.pallas_call(
        tables_kernel,
        out_shape=(
            jax.ShapeDtypeStruct((8, 3 * L), jnp.int32),
            jax.ShapeDtypeStruct((PAD, C), BF16),
            jax.ShapeDtypeStruct((ROWS, C), BF16),
            jax.ShapeDtypeStruct((4, PAD, PAD), F32),
        ),
        in_specs=[vmem] * 8,
        out_specs=(vmem,) * 4,
        scratch_shapes=[
            pltpu.VMEM((8, L), jnp.int32),
            pltpu.VMEM((3, 8, L), jnp.int32),
            pltpu.VMEM((2, 8, C), F32),
            pltpu.VMEM((4, 8, 384), F32),
            pltpu.VMEM((8, 8, 384), F32),
            pltpu.VMEM((2, 8, C), F32),
            pltpu.VMEM((PAD, C), BF16),
            pltpu.VMEM((PAD, C), BF16),
            pltpu.VMEM((ROWS, PAD), F32),
            pltpu.VMEM((128, 384), F32),
            pltpu.VMEM((4, 32, 384), F32),
            pltpu.VMEM((32, 384), F32),
            pltpu.VMEM((8, 8, 384), F32),
            pltpu.VMEM((4, 8, 384), F32),
            pltpu.VMEM((ROWS, C), BF16),
            pltpu.SemaphoreType.DMA((2, 3)),
            pltpu.SemaphoreType.DMA((40,)),
            pltpu.SemaphoreType.DMA((40,)),
        ],
        compiler_params=pltpu.CompilerParams(
            collective_id=0, has_side_effects=True, vmem_limit_bytes=40 * 2**20
        ),
        name="tables",
    )(tokens, embed, k1, g1, w1, k2, g2, w2)


BLOCK = 256
BLOCKS = C // BLOCK


def code_of(left, middle, right):
    code = jnp.where(
        left == 4,
        64 + 4 * middle + right,
        jnp.where(right == 4, 80 + 4 * left + middle, 16 * left + 4 * middle + right),
    )
    return jnp.where(middle == 4, -1, code)


def tap_index(codes):
    first, second, third = codes
    second = jnp.where(second < 0, -1, 80 + second)
    third = jnp.where(third < 0, -1, jnp.where(third < 64, 176 + third, 160 + third))
    return first, second, third


def rows_kernel(
    ext_ref,
    m_ref,
    p_ref,
    k2_ref,
    cot_ref,
    out_ref,
    x_ref,
    hot,
    hot_t,
    wide_a,
    wide_b,
    mid_t,
    cots,
    mids,
    fins,
    preu,
    slope,
    acc,
    acc2,
):
    ext = ext_ref[...]
    left = pltpu.roll(ext, FIRST_DILATE, 1)
    right = pltpu.roll(ext, 3 * L - FIRST_DILATE, 1)

    def other(base):
        return jnp.where(base == 4, 4, 3 - base)

    start = L - SECOND_DILATE
    code_a = pltpu.roll(code_of(left, ext, right), 3 * L - start, 1)[:, 0:384]
    code_b = pltpu.roll(code_of(other(right), other(ext), other(left)), 3 * L - start, 1)[:, 0:384]

    def shifts(code):
        return [code[:, 0:L]] + [
            pltpu.roll(code, 384 - s, 1)[:, 0:L] for s in (SECOND_DILATE, 2 * SECOND_DILATE)
        ]

    three_a = shifts(code_a)
    three_b = shifts(code_b)[::-1]
    index = [jnp.concatenate([a, b], axis=1) for a, b in zip(tap_index(three_a), tap_index(three_b))]
    line = iota((ROWS, 2 * L), 0)
    hit = (line == index[0][0:1]) | (line == index[1][0:1]) | (line == index[2][0:1])
    hot_t[...] = jnp.where(hit, 1.0, 0.0).astype(BF16)
    mid_t[...] = jnp.where(
        iota((PAD, 2 * L), 0) == jnp.concatenate([three_a[1], three_b[1]], axis=1)[0:1], 1.0, 0.0
    ).astype(BF16)

    def column(row):
        return jnp.transpose(row.astype(F32))[:, 0:1].astype(jnp.int32)

    columns = [column(row) for row in index]
    line = iota((2 * L, ROWS), 1)
    hit = (line == columns[0]) | (line == columns[1]) | (line == columns[2])
    hot[...] = jnp.where(hit, 1.0, 0.0).astype(BF16)
    line = iota((384, PAD), 1)
    wide_a[...] = jnp.where(line == column(code_a), 1.0, 0.0).astype(BF16)
    wide_b[...] = jnp.where(line == column(code_b), 1.0, 0.0).astype(BF16)

    mirror = jnp.where(
        iota((BLOCK, BLOCK), 0) + iota((BLOCK, BLOCK), 1) == BLOCK - 1, 1.0, 0.0
    ).astype(BF16)

    acc[...] = jnp.zeros_like(acc)
    acc2[...] = jnp.zeros_like(acc2)

    def first_pass(b, carry):
        here = lanes(b, BLOCK)
        there = lanes(BLOCKS - 1 - b, BLOCK)
        cots[0:L, here] = cot_ref[:, here]
        cots[L : 2 * L, here] = dot(cot_ref[:, there], mirror).astype(BF16)
        m = m_ref[:, here]
        taps = k2_ref[:, here]
        for n, (wide, order) in enumerate(((wide_a, (0, 1, 2)), (wide_b, (2, 1, 0)))):
            mid = dot(wide[...], m)
            conv = (
                taps[order[0] : order[0] + 1] * mid[0:L]
                + taps[order[1] : order[1] + 1] * mid[64 : 64 + L]
                + taps[order[2] : order[2] + 1] * mid[128 : 128 + L]
            )
            square = conv * conv
            acc[n * L : n * L + L] += square[:, 0:128] + square[:, 128:256]
            mids[n * L : n * L + L, here] = mid[64 : 64 + L].astype(BF16)
        return carry

    lax.fori_loop(0, BLOCKS, first_pass, 0)
    acc[...] = jnp.broadcast_to(
        lax.rsqrt(jnp.sum(acc[...], axis=1, keepdims=True) * (1.0 / C) + EPS), (2 * L, 128)
    )

    def second_pass(b, carry):
        here = lanes(b, BLOCK)
        preu[...] = dot(hot[...], p_ref[:, here])

        def chunk(r, carry):
            some = rows(r, 64)
            inv = acc[some][:, 0:1]
            pre = inv * preu[some]
            act, grad = gelu_parts(pre)
            fins[some, here] = (mids[some, here].astype(F32) + act).astype(BF16)
            sl = cots[some, here].astype(F32) * grad
            prod = sl * pre
            acc2[some] += prod[:, 0:128] + prod[:, 128:256]
            slope[some] = (inv * sl).astype(BF16)
            return carry

        lax.fori_loop(0, 8, chunk, 0)
        x_ref[:, here] = 0.5 * dot(hot_t[...], slope[...])
        return carry

    lax.fori_loop(0, BLOCKS, second_pass, 0)

    def third_pass(b, carry):
        here = lanes(b, BLOCK)
        there = lanes(BLOCKS - 1 - b, BLOCK)
        far = dot(fins[L : 2 * L, there], mirror)
        out_ref[:, here] = (0.5 * (fins[0:L, here].astype(F32) + far)).astype(BF16)
        return carry

    lax.fori_loop(0, BLOCKS, third_pass, 0)

    inv = acc[:, 0:1]
    weight = (0.5 / C) * inv * inv * jnp.sum(acc2[...], axis=1, keepdims=True)
    high, low = split(weight * hot[...].astype(F32))
    x_ref[:, C : C + ROWS] = dot(hot_t[...], high) + dot(hot_t[...], low)
    x_ref[192:256, C + ROWS : WIDE] = jnp.zeros((64, WIDE - C - ROWS), F32)
    for n in range(2):
        v = 0.5 * dot(mid_t[...], cots[:, 768 * n : 768 * n + 768])
        x_ref[CODES * n : CODES * n + CODES, C + ROWS : WIDE] = v[0:CODES]


def row_work(ext, m, p, k2, cot):
    vmem = pl.BlockSpec(memory_space=pltpu.VMEM)
    return pl.pallas_call(
        rows_kernel,
        out_shape=(
            jax.ShapeDtypeStruct((L, C), BF16),
            jax.ShapeDtypeStruct((ROWS, WIDE), F32),
        ),
        in_specs=[vmem] * 5,
        out_specs=(vmem,) * 2,
        scratch_shapes=[
            pltpu.VMEM((2 * L, ROWS), BF16),
            pltpu.VMEM((ROWS, 2 * L), BF16),
            pltpu.VMEM((384, PAD), BF16),
            pltpu.VMEM((384, PAD), BF16),
            pltpu.VMEM((PAD, 2 * L), BF16),
            pltpu.VMEM((2 * L, C), BF16),
            pltpu.VMEM((2 * L, C), BF16),
            pltpu.VMEM((2 * L, C), BF16),
            pltpu.VMEM((2 * L, BLOCK), F32),
            pltpu.VMEM((2 * L, BLOCK), BF16),
            pltpu.VMEM((2 * L, 128), F32),
            pltpu.VMEM((2 * L, 128), F32),
        ],
        compiler_params=pltpu.CompilerParams(vmem_limit_bytes=40 * 2**20),
        name="rows",
    )(ext, m, p, k2, cot)


QUART = WIDE // 4


def tail_kernel(
    x_ref,
    own_ref,
    w1_ref,
    w2_ref,
    gwa_ref,
    gwb_ref,
    vec_ref,
    from_core,
    half_sum,
    half_low,
    xin,
    xsum,
    yin,
    ysum,
    zin,
    zmid,
    full,
    wpad1,
    wpad2,
    pack,
    packs,
    fbuf,
    pack2,
    packs2,
    send,
    recv,
):
    y, z, x, c = coords()
    pos = lax.axis_index("pos")
    barrier = pltpu.get_barrier_semaphore()
    peers = axis_peers()
    for peer in peers:
        pl.semaphore_signal(barrier, inc=1, device_id=peer, device_id_type=MESH)
    wpad1[...] = jnp.zeros_like(wpad1)
    wpad2[...] = jnp.zeros_like(wpad2)
    wpad1[0:OWN] = w1_ref[...]
    wpad2[0:OWN] = w2_ref[...]
    pl.semaphore_wait(barrier, len(peers))

    net = Sender(send, recv)
    half = rows(c, 128)
    finish([net.start(x_ref.at[rows(1 - c, 128)], from_core, other_core())])
    half_sum[...] = x_ref[half] + from_core[...]
    half_low[...] = half_sum[...].astype(BF16)
    copies = [
        net.start(half_low.at[rows((x + d) % 4, 32)], xin.at[d - 1], along_x(d))
        for d in range(1, 4)
    ]
    finish(copies)
    xsum[...] = (
        half_sum[rows(x, 32)] + xin[0].astype(F32) + xin[1].astype(F32) + xin[2].astype(F32)
    )
    copies = [
        net.start(xsum.at[:, lanes((y + d) % 4, QUART)], yin.at[d - 1], along_y(d))
        for d in range(1, 4)
    ]
    finish(copies)
    quart = lanes(y, QUART)
    ysum[...] = xsum[:, quart] + yin[0] + yin[1] + yin[2]
    copies = [
        net.start(ysum.at[rows((z + d) % 4, 8)], zin.at[z], along_z(d)) for d in range(1, 8)
    ]
    zin[z] = ysum[rows(z % 4, 8)]
    finish(copies)
    total = zin[0]
    for i in range(1, 8):
        total = total + zin[i]
    zmid[z % 4] = total
    finish([net.start(zmid.at[z % 4], zmid.at[z % 4], along_half_z(d)) for d in range(1, 4)])
    third = pl.ds(pl.multiple_of(c * 128 + x * 32, 32), 32)
    full[third, quart] = jnp.concatenate([zmid[i] for i in range(4)], axis=0).astype(BF16)
    block = full.at[third, quart]
    finish([net.start(block, block, along_y(d)) for d in range(1, 4)])
    block = full.at[third]
    finish([net.start(block, block, along_x(d)) for d in range(1, 4)])
    block = full.at[half]
    finish([net.start(block, block, other_core())])

    pre, inv, m_own = own_ref[0], own_ref[1], own_ref[2]
    vec = own_ref[3, 0:16]
    e_own, g1, g2 = vec[0:4], vec[7:8], vec[11:12]
    taps = [vec[8 + k : 9 + k] for k in range(3)]
    b_own = tap_rows(taps, m_own)
    energy = full[:, 0:C]
    ew = dot_nt(energy, wpad2[...])
    high, low = split(b_own)
    gram = full[:, C : C + ROWS]
    d = g2 * ew - (dot(gram, high) + dot(gram, low))
    m0, m1 = m_own[0:64], m_own[64:80]
    m2 = m_own[80:96]

    def total_rows(value):
        return jnp.sum(value, axis=0, keepdims=True)

    taps_b = [
        total_rows(m_own[0:80] * d[0:80]),
        total_rows(m_own[0:96] * d[80:176]),
        total_rows(m0 * d[176:240]) + total_rows(m2 * d[240:256]),
    ]
    gain_b = total_rows(b_own * ew)
    pick = jnp.where(
        (iota((C, PAD), 0) == pos * OWN + iota((C, PAD), 1)) & (iota((C, PAD), 1) < OWN), 1.0, 0.0
    ).astype(BF16)
    v = dot(full[0:CODES, C + ROWS : WIDE], pick[0:768]) + dot(
        full[CODES : 2 * CODES, C + ROWS : WIDE], pick[768:C]
    )
    up = v + taps[1] * d[80:176]
    up = up + jnp.concatenate(
        [taps[0] * d[0:64] + taps[2] * d[176:240], taps[0] * d[64:80], taps[2] * d[240:256]],
        axis=0,
    )
    _, slope = gelu_parts(pre[0:CODES])
    s = slope * up
    a = jnp.sum(s * pre[0:CODES], axis=1, keepdims=True) * (1.0 / C)
    inv = inv[0:CODES]
    hot_t = code_onehot(iota((16, CODES), 1), iota((16, CODES), 0))
    hot_far = code_onehot(iota((CODES, PAD), 0), iota((CODES, PAD), 1) - 64)
    f = dot(hot_t, inv * s, HIGH)
    gram_a = dot(hot_t, (inv * inv * a) * hot_far, HIGH)
    pack_rows = jnp.concatenate([jnp.zeros((12, PAD), F32)] + taps_b + [gain_b], axis=0)
    packet = f + gram_a + pack_rows
    pack[0] = packet[0:8]
    pack[1] = packet[8:16]
    packs[c, z, y] = pack[c]
    copies = [net.start(pack.at[c], packs.at[c, z, y], along_y(d)) for d in range(1, 4)]

    a_own = g2 * b_own
    high, low = split(jnp.transpose(a_own))
    finish(copies)
    block = packs.at[c, z]
    copies = [net.start(block, block, along_z(d)) for d in range(1, 8)]
    both = jnp.concatenate([high[0:OWN], low[0:OWN]], axis=0)
    for b in range(0, C, 512):
        grad = dot(both, full[:, b : b + 512])
        gwb_ref[:, b : b + 512] = grad[0:OWN] + grad[OWN : 2 * OWN]
    finish(copies)
    block = packs.at[c]
    finish([net.start(block, block, other_core())])

    gram_a = jnp.zeros((16, PAD), F32)
    fbuf[...] = jnp.zeros_like(fbuf)
    for i in range(32):
        for h in range(2):
            fbuf[8 * h : 8 * h + 8, OWN * i : OWN * i + OWN] = packs[h, i % 8, i // 8][:, 0:OWN]
        gram_a = gram_a + jnp.concatenate(
            [packs[0, i % 8, i // 8], packs[1, i % 8, i // 8]], axis=0
        )
    f = fbuf[0:16]
    te_own = jnp.concatenate(
        [vec[4 + k : 5 + k] * e_own for k in range(3)] + [jnp.zeros((4, PAD), F32)], axis=0
    )
    high, low = split(f)
    fw = dot_nt(jnp.concatenate([high, low], axis=0), wpad1[...])
    fw = fw[0:16] + fw[16:32]
    spread = jnp.concatenate(
        [jnp.zeros((64, PAD), F32), te_own, jnp.zeros((48, PAD), F32)], axis=0
    )
    far = jnp.where(iota((16, PAD), 1) >= 64, gram_a, 0.0)
    da = g1 * fw - dot(far, spread, HIGH)
    rows_a = [total_rows(e_own * da[4 * k : 4 * k + 4]) for k in range(3)]
    rows_a = rows_a + [total_rows(te_own * fw), jnp.zeros((4, PAD), F32)]
    pack2[...] = jnp.concatenate(rows_a, axis=0)
    packs2[z, y] = pack2[...]
    copies = [net.start(pack2, packs2.at[z, y], along_y(d)) for d in range(1, 4)]

    wide = jnp.concatenate([g1 * te_own, jnp.zeros((PAD - 16, PAD), F32)], axis=0)
    wide = jnp.transpose(wide)
    finish(copies)
    block = packs2.at[z]
    copies = [net.start(block, block, along_z(d)) for d in range(1, 8)]
    for b in range(0, C, 512):
        gwa_ref[:, b : b + 512] = dot(wide, fbuf[:, b : b + 512], HIGH)[0:OWN]
    finish(copies)
    for i in range(32):
        vec_ref[0:4, OWN * i : OWN * i + OWN] = packs2[i % 8, i // 8][0:4, 0:OWN]
    vec_ref[4:8, :] = fbuf[12:16, :]


def tail(x, own, w1, w2):
    vmem = pl.BlockSpec(memory_space=pltpu.VMEM)
    return pl.pallas_call(
        tail_kernel,
        out_shape=(
            jax.ShapeDtypeStruct((OWN, C), F32),
            jax.ShapeDtypeStruct((OWN, C), F32),
            jax.ShapeDtypeStruct((8, C), F32),
        ),
        in_specs=[vmem] * 4,
        out_specs=(vmem,) * 3,
        scratch_shapes=[
            pltpu.VMEM((128, WIDE), F32),
            pltpu.VMEM((128, WIDE), F32),
            pltpu.VMEM((128, WIDE), BF16),
            pltpu.VMEM((3, 32, WIDE), BF16),
            pltpu.VMEM((32, WIDE), F32),
            pltpu.VMEM((3, 32, QUART), F32),
            pltpu.VMEM((32, QUART), F32),
            pltpu.VMEM((8, 8, QUART), F32),
            pltpu.VMEM((4, 8, QUART), F32),
            pltpu.VMEM((ROWS, WIDE), BF16),
            pltpu.VMEM((PAD, C), BF16),
            pltpu.VMEM((PAD, C), BF16),
            pltpu.VMEM((2, 8, PAD), F32),
            pltpu.VMEM((2, 8, 4, 8, PAD), F32),
            pltpu.VMEM((PAD, C), F32),
            pltpu.VMEM((8, PAD), F32),
            pltpu.VMEM((8, 4, 8, PAD), F32),
            pltpu.SemaphoreType.DMA((52,)),
            pltpu.SemaphoreType.DMA((52,)),
        ],
        compiler_params=pltpu.CompilerParams(
            collective_id=1, has_side_effects=True, vmem_limit_bytes=40 * 2**20
        ),
        name="tail",
    )(x, own, w1, w2)


def shards(tokens, embed, k1, g1, w1, k2, g2, w2, cotangent):
    ext, m, p, own = tables(
        tokens, embed, k1, g1.reshape(1, C), w1, k2, g2.reshape(1, C), w2
    )
    out, x = row_work(ext, m, p, k2, cotangent[0, 0])
    gwa, gwb, vec = tail(x, own, w1, w2)
    return (out[None, None], gwa, gwb, vec[0:3], vec[4:7], vec[3], vec[7])


def solution(mesh):
    placed = (
        P("rep", "pos"),
        P(),
        P(),
        P(),
        P("pos", None),
        P(),
        P(),
        P("pos", None),
        P("rep", "strand", "pos", None),
    )
    return jax.shard_map(
        shards,
        mesh=mesh,
        in_specs=placed,
        out_specs=(
            P("rep", "strand", "pos", None),
            P("pos", None),
            P("pos", None),
            P(),
            P(),
            P(),
            P(),
        ),
        check_vma=False,
    )
```

time: 1040 us -> 146 us (0.14)
  waiting for transfers between devices: 789 us -> 0 us
  Pallas kernels: 0 us -> 132 us
  blocking collectives: 118 us -> 0 us
  matrix products: 37.6 us -> 0 us
  starting transfers between devices: 25.4 us -> 0 us
  local copies, waits for them, and re-layouts: 36 us -> 11.7 us
  other arithmetic: 15.7 us -> 0 us
  between operations: 14.3 us -> 0.67 us
    reduce_scatter x2 -> x0, waiting for transfers between devices: 411 us -> none  [weight_grad(): lax.psum_scatter(lax.dot_general(normed, slopes, (((0,), (0,)), ((), ()))...]
    ppermute x12 -> x0, waiting for transfers between devices: 271 us -> none  [the longest x6 264 us: swapped(): return lax.ppermute(value, axis, pairs)]
    pallas_call x0 -> x3, Pallas kernels: none -> 132 us  [the longest x1 65.2 us: tail(): pl.pallas_call(tail_kernel, out_shape=(jax.ShapeDtypeStruct((OWN, C), F32...]
    all_gather x2 -> x0, waiting for transfers between devices: 106 us -> none  [the longest x1 67.3 us: shards(): lax.all_gather(second_weight, 'pos', axis=0, tiled=True)]
    psum x1 -> x0, blocking collectives: 79.5 us -> none  [shards(): lax.psum((first_kernel_share, first_gain_share, second_kernel_share, seco...]
    all_gather x1 -> x0, blocking collectives: 38.4 us -> none  [shards(): whole_tokens = lax.all_gather(own_tokens, 'pos', axis=0, tiled=True)]
    dot_general x7 -> x0, matrix products: 37.6 us -> none  [the longest x2 13.2 us: weight_grad(): lax.dot_general(normed, slopes, (((0,), (0,)), ((), ())), preferred_eleme...]
    rev x3 -> x0, local copies, waits for them, and re-layouts: 25.3 us -> none  [the longest x1 12.6 us: shards(): cot_far[::-1, ::-1].astype(jnp.float32)]
  transfers between devices with their start and end apart: 17 -> 0, of which waited for: 16 -> 0; matrix products, arithmetic and copies ran while one was open for 5% -> 0% of each run, Pallas kernels for 0% -> 0%
where the time goes in v1:
time: 146 us; the launch traced here: 144 us
  Pallas kernels  132 us (90%)
  local copies, waits for them, and re-layouts  11.7 us (8%)
    pallas_call x1, Pallas kernels, tail(): pl.pallas_call(tail_kernel, out_shape=(jax.ShapeDtypeStruct((OWN, C), F32...  65.2 us
    pallas_call x1, Pallas kernels, tables(): pl.pallas_call(tables_kernel, out_shape=(jax.ShapeDtypeStruct((8, 3 * L),...  51.6 us
    pallas_call x1, Pallas kernels, row_work(): pl.pallas_call(rows_kernel, out_shape=(jax.ShapeDtypeStruct((L, C), BF16)...  14.9 us
    unnamed x20, local copies, waits for them, and re-layouts  9.05 us

profile of v1, /device:TPU:1, one launch (start us, length us, event | category | flops | bytes accessed | tf_op | source)
XLA Modules:
  0.0 144.1 jit_solution(17748153943349102910)
XLA Ops:
  0.6 0.7 reshape.20.g1_ref
  1.3 0.7 reshape.21.g2_ref
  2.0 0.0 copy-start.1
  2.0 0.9 copy-done.1
  2.9 0.0 copy-start.3
  2.9 0.9 copy-done.3
  3.9 0.0 copy-start.5
  3.9 0.7 copy-done.5
  4.6 0.0 copy-start.6
  4.6 0.7 copy-done.6
  5.3 0.0 copy-start.7
  5.3 0.7 copy-done.7
  6.0 0.0 copy-start.8
  6.0 0.7 copy-done.8
  6.7 51.6 %tables.1 = (s32[8,768]{1,0:T(8,128)S(1)}, bf16[128,1536]{1,0:T(8,128)(2,1)S(1)}, bf16[256,1536]{1,0:T(8,128)(2,1)S(1)}, f32[4,128,128]{2,1,0:T(8,128)S(1)}) custom-call(s32[1,256]{1,0:T(1,128)S(1)} %copy-done.8, bf16[4,1536]{1,0:T(4,128)(2,1)S(1)} %copy-done.7, f32[3,1536]{1,0:T(4,128)S(1)} %copy-done.6, f32[1,1536]{1,0:T(1,128)S(1)} %reshape.20.g1_ref, ...), custom_call_target="tpu_custom_call" | custom-call | tf_op jit(solution)/shard_map/tables/pallas_call | solution.py:346
  58.3 0.0 copy-start
  58.3 1.1 copy-done
  59.5 14.9 %rows.1 = (bf16[256,1536]{1,0:T(8,128)(2,1)}, f32[256,2560]{1,0:T(8,128)S(1)}) custom-call(s32[8,768]{1,0:T(8,128)S(1)} %get-tuple-element.16.ext_ref, bf16[128,1536]{1,0:T(8,128)(2,1)S(1)} %get-tuple-element.17.m_ref, bf16[256,1536]{1,0:T(8,128)(2,1)S(1)} %get-tuple-element.18.p_ref, f32[3,1536]{1,0:T(4,128)S(1)} %copy-done.5, bf16[256,1536]{1,0:T(8,128)(2,1)S(1)} %bitcast.2), custom_call_target="tpu_custom_call" | custom-call | tf_op jit(solution)/shard_map/rows/pallas_call | solution.py:535
  74.4 0.0 copy-start.2
  74.4 0.9 copy-done.2
  75.3 0.0 copy-start.4
  75.3 0.9 copy-done.4
  76.2 65.2 %tail.1 = (f32[48,1536]{1,0:T(8,128)S(1)}, f32[48,1536]{1,0:T(8,128)S(1)}, f32[8,1536]{1,0:T(8,128)S(1)}) custom-call(f32[256,2560]{1,0:T(8,128)S(1)} %get-tuple-element.20.x_ref, f32[4,128,128]{2,1,0:T(8,128)S(1)} %get-tuple-element.21.own_ref, bf16[48,1536]{1,0:T(8,128)(2,1)S(1)} %copy-done.2, bf16[48,1536]{1,0:T(8,128)(2,1)S(1)} %copy-done.4), custom_call_target="tpu_custom_call" | custom-call | tf_op jit(solution)/shard_map/tail/pallas_call | solution.py:746
  141.5 0.6 slice_reduce_fusion
  142.1 0.6 fusion
  142.7 0.7 copy.18
  143.4 0.7 copy.19
Async XLA Ops:
  2.0 0.9 copy-start.1
  2.9 0.9 copy-start.3
  3.9 0.7 copy-start.5
  4.6 0.7 copy-start.6
  5.3 0.7 copy-start.7
  6.0 0.7 copy-start.8
  58.3 1.1 copy-start
  74.4 0.9 copy-start.2
  75.3 0.9 copy-start.4

commit v2 on v0

v2 whole, which is shorter than its diff:
```python
import functools

import jax
import jax.numpy as jnp
from jax import lax
from jax.experimental import pallas as pl
from jax.experimental.pallas import tpu as pltpu
from jax.sharding import PartitionSpec as P

MESH = pl.DeviceIdType.MESH
HIGH = lax.Precision.HIGHEST
F32 = jnp.float32
BF16 = jnp.bfloat16
C = 1536
L = 256
FIRST_DILATE = 32
SECOND_DILATE = 64
EPS = 1e-05
CODES = 96
PAD = 128
ROWS = 256
WIDE = 2048
QUART = WIDE // 4
BLOCK = 256
BLOCKS = C // BLOCK
OWN = 48
GELU_A = 0.7978845608028654
GELU_B = 0.044715


def coords():
    pos = lax.axis_index("pos")
    strand = lax.axis_index("strand")
    rep = lax.axis_index("rep")
    return pos // 8, pos % 8, (rep // 2) * 2 + strand, rep % 2


def device(y, z, x, c):
    return {"pos": y * 8 + z, "strand": x % 2, "rep": (x // 2) * 2 + c}


def along_y(d):
    y, z, x, c = coords()
    return device((y + d) % 4, z, x, c)


def along_z(d):
    y, z, x, c = coords()
    return device(y, (z + d) % 8, x, c)


def along_half_z(d):
    y, z, x, c = coords()
    return device(y, (z // 4) * 4 + (z + d) % 4, x, c)


def other_core():
    y, z, x, c = coords()
    return device(y, z, x, 1 - c)


PLANE = [(a, b) for a in range(4) for b in range(8) if a or b]
SQUARE = [(a, b) for a in range(4) for b in range(4) if a or b]


def in_plane(a, b):
    y, z, x, c = coords()
    return device((y + a) % 4, (z + b) % 8, x, c)


def in_square(a, b):
    y, z, x, c = coords()
    return device((y + b) % 4, z, (x + a) % 4, c)


class Net:
    def __init__(self, send, recv):
        self.send, self.recv, self.used = send, recv, 0

    def take(self, count):
        first = self.used
        self.used += count
        return first

    def copy(self, src, dst, to, sem):
        return pltpu.make_async_remote_copy(
            src_ref=src,
            dst_ref=dst,
            send_sem=self.send.at[sem],
            recv_sem=self.recv.at[sem],
            device_id=to,
            device_id_type=MESH,
        )

    def start(self, src, dst, to):
        copy = self.copy(src, dst, to, self.take(1))
        copy.start()
        return copy


def finish(copies):
    for copy in copies:
        copy.wait()


def lanes(index, width):
    return pl.ds(pl.multiple_of(index * width, 128), width)


def rows(index, height):
    return pl.ds(pl.multiple_of(index * height, 8), height)


def dot(a, b, precision=None):
    return lax.dot_general(
        a, b, (((1,), (0,)), ((), ())), preferred_element_type=F32, precision=precision
    )


def dot_nt(a, b):
    return lax.dot_general(a, b, (((1,), (1,)), ((), ())), preferred_element_type=F32)


def split(value):
    high = value.astype(BF16)
    return high, (value - high.astype(F32)).astype(BF16)


def gelu_parts(pre):
    square = pre * pre
    th = jnp.tanh(GELU_A * pre * (1.0 + GELU_B * square))
    half = 0.5 * (1.0 + th)
    slope = half + 0.5 * pre * (1.0 - th * th) * (GELU_A * (1.0 + 3.0 * GELU_B * square))
    return pre * half, slope


def code_bases(code):
    inner, left = code < 64, code < 80
    one = jnp.where(inner, code // 16, jnp.where(left, -1, (code - 80) // 4))
    two = jnp.where(inner, (code // 4) % 4, jnp.where(left, (code - 64) // 4, code % 4))
    three = jnp.where(inner | left, code % 4, -1)
    return one, two, three


def code_onehot(code, column):
    one, two, three = code_bases(code)
    hit = (column == one) & (one >= 0)
    hit = hit | (column == 4 + two) | ((column == 8 + three) & (three >= 0))
    return jnp.where(hit & (code < CODES), 1.0, 0.0)


def iota(shape, axis):
    return lax.broadcasted_iota(jnp.int32, shape, axis)


def tap_rows(taps, table):
    return jnp.concatenate(
        [taps[0] * table[0:80], taps[1] * table[0:96], taps[2] * table[0:64], taps[2] * table[80:96]],
        axis=0,
    )


def code_of(left, middle, right):
    code = jnp.where(
        left == 4,
        64 + 4 * middle + right,
        jnp.where(right == 4, 80 + 4 * left + middle, 16 * left + 4 * middle + right),
    )
    return jnp.where(middle == 4, -1, code)


def tap_index(codes):
    first, second, third = codes
    second = jnp.where(second < 0, -1, 80 + second)
    third = jnp.where(third < 0, -1, jnp.where(third < 64, 176 + third, 160 + third))
    return first, second, third


def whole_kernel(
    tok_in,
    emb_in,
    k1_in,
    g1_in,
    w1_in,
    k2_in,
    g2_in,
    w2_in,
    cot_in,
    out_out,
    gw_ref,
    vec_ref,
    tok,
    emb16,
    k1_ref,
    g1_ref,
    k2_ref,
    g2_ref,
    wpad1,
    wpad2,
    cot,
    tsend,
    trecv,
    qsend,
    qrecv,
    qown,
    qparts,
    qfull,
    aown,
    ppart,
    py,
    psum,
    pz,
    pmid,
    pbuf,
    table,
    table_slope,
    table_v,
    hot,
    hot_t,
    wide_a,
    wide_b,
    mid_t,
    cots,
    mids,
    fins,
    preu,
    slope,
    acc,
    acc2,
    out_buf,
    xbuf,
    core_send,
    from_core,
    chip_low,
    xin,
    xsum,
    zin,
    zout,
    full,
    pack,
    packs,
    fbuf,
    pack2,
    packs2,
    lsem,
    tsem,
    send,
    recv,
):
    y, z, x, c = coords()
    pos = lax.axis_index("pos")
    strand = lax.axis_index("strand")
    rep = lax.axis_index("rep")
    frame = jnp.where(strand == 1, 31 - pos, pos)
    targets = [(frame + d + 32) % 32 for d in (-1, 0, 1)]
    net = Net(send, recv)

    wpad1[OWN:PAD] = jnp.zeros((PAD - OWN, C), BF16)
    wpad2[OWN:PAD] = jnp.zeros((PAD - OWN, C), BF16)
    loads = [
        pltpu.make_async_copy(src, dst, lsem.at[i])
        for i, (src, dst) in enumerate(
            (
                (emb_in, emb16),
                (k1_in, k1_ref),
                (g1_in, g1_ref),
                (w1_in, wpad1.at[0:OWN]),
                (k2_in, k2_ref),
                (g2_in, g2_ref),
                (tok_in, tok),
                (w2_in, wpad2.at[0:OWN]),
                (cot_in, cot),
            )
        )
    ]
    for load in loads:
        load.start()

    barrier = pltpu.get_barrier_semaphore()
    peers = (
        [in_plane(a, b) for a, b in PLANE]
        + [in_square(a, b) for a, b in SQUARE if a]
        + [other_core()]
    )
    for peer in peers:
        pl.semaphore_signal(barrier, inc=1, device_id=peer, device_id_type=MESH)

    for load in loads[:7]:
        load.wait()
    tokens = jnp.broadcast_to(tok[...], (8, L)).astype(F32)
    flip = jnp.where(iota((L, L), 0) + iota((L, L), 1) == L - 1, 1.0, 0.0)
    turned = 3.0 - dot(tokens, flip)
    tsend[...] = jnp.where(strand == 1, turned, tokens).astype(jnp.int32)
    emb = emb16[...].astype(F32)
    k1, k2 = k1_ref[...], k2_ref[...]
    g1, g2 = g1_ref[...], g2_ref[...]
    packed = jnp.concatenate([emb, k1, g1, k2, g2, jnp.zeros((4, C), F32)], axis=0)
    vec = pltpu.roll(packed, lax.rem(C - pos * OWN, C), 1)[:, 0:PAD]
    vec = jnp.where(iota((16, PAD), 1) < OWN, vec, 0.0)
    e_own, g1_own, g2_own = vec[0:4], vec[7:8], vec[11:12]
    taps = [vec[8 + k : 9 + k] for k in range(3)]
    te_own = jnp.concatenate(
        [vec[4 + k : 5 + k] * e_own for k in range(3)] + [jnp.zeros((4, PAD), F32)], axis=0
    )
    high, low = split(g1_own * te_own)
    part = dot(jnp.concatenate([high, low], axis=0), wpad1[...])
    part = part[0:16] + part[16:32]
    qsend[...] = jnp.zeros_like(qsend)
    for i in range(32):
        qsend[i, :, 0:OWN] = part[0:8, OWN * i : OWN * i + OWN]
        qsend[i, :, 64 : 64 + OWN] = part[8:16, OWN * i : OWN * i + OWN]
    qrecv[pos] = qsend[pos]

    pl.semaphore_wait(barrier, len(peers))

    def token_copy(j):
        return pltpu.make_async_remote_copy(
            src_ref=tsend,
            dst_ref=trecv.at[2 - j],
            send_sem=tsem.at[0, j],
            recv_sem=tsem.at[1, j],
            device_id={"pos": targets[j], "strand": strand, "rep": rep},
            device_id_type=MESH,
        )

    for j in range(3):
        @pl.when(targets[j] != pos)
        def _():
            token_copy(j).start()

        @pl.when(targets[j] == pos)
        def _():
            trecv[2 - j] = tsend[...]

    q_copies = []
    for a, b in PLANE:
        there = ((y + a) % 4) * 8 + (z + b) % 8
        q_copies.append(net.start(qsend.at[there], qrecv.at[pos], in_plane(a, b)))

    te = jnp.concatenate([k1[k : k + 1] * emb for k in range(3)] + [jnp.zeros((4, C), F32)], axis=0)
    hot_code = code_onehot(iota((PAD, 16), 0), iota((PAD, 16), 1))
    conv = dot(hot_code, te, HIGH)
    inv_a = lax.rsqrt(jnp.mean(conv * conv, axis=-1, keepdims=True) + EPS)

    mirror = jnp.where(
        iota((BLOCK, BLOCK), 0) + iota((BLOCK, BLOCK), 1) == BLOCK - 1, 1.0, 0.0
    ).astype(BF16)
    loads[7].wait()
    loads[8].wait()

    def turn_cot(b, carry):
        here = lanes(b, BLOCK)
        there = lanes(BLOCKS - 1 - b, BLOCK)
        cots[0:L, here] = cot[:, here]
        cots[L : 2 * L, here] = dot(cot[:, there], mirror).astype(BF16)
        return carry

    lax.fori_loop(0, BLOCKS, turn_cot, 0)

    finish(q_copies)
    total = qrecv[0]
    for i in range(1, 32):
        total = total + qrecv[i]
    qown[...] = total
    qparts[pos] = total
    q_copies = [net.start(qown, qparts.at[pos], in_plane(a, b)) for a, b in PLANE]

    q_two = jnp.concatenate([total, pltpu.roll(total, 64, 1)], axis=0)
    q_two = jnp.where(iota((16, PAD), 1) < OWN, q_two, 0.0)
    pre_own = inv_a * dot(hot_code, q_two, HIGH)
    act, slope_own = gelu_parts(pre_own)
    pads = jnp.zeros((4, PAD), F32)
    center = dot(hot_code, jnp.concatenate([pads, e_own, pads, pads], axis=0), HIGH)
    m_own = jnp.where(iota((PAD, PAD), 0) < CODES, center + act, 0.0)
    m_own = m_own.astype(BF16).astype(F32)
    b_own = tap_rows(taps, m_own)
    a_own = g2_own * b_own
    aown[...] = a_own
    high, low = split(aown[rows(c, 128)])
    mine = lanes(x, 384)
    w2 = wpad2[:, mine]
    ppart[...] = dot(high, w2) + dot(low, w2)
    p_copies = [
        net.start(ppart.at[rows((y + d) % 4, 32)], py.at[d - 1], along_y(d)) for d in range(1, 4)
    ]

    for j in range(3):
        @pl.when(targets[j] != pos)
        def _():
            token_copy(j).wait()
    joined = jnp.concatenate([trecv[0], trecv[1], trecv[2]], axis=1)
    place = (pos - 1) * L + iota((8, 3 * L), 1)
    ext = jnp.where((place >= 0) & (place < 32 * L), joined, 4)
    left = pltpu.roll(ext, FIRST_DILATE, 1)
    right = pltpu.roll(ext, 3 * L - FIRST_DILATE, 1)

    def other(base):
        return jnp.where(base == 4, 4, 3 - base)

    start = L - SECOND_DILATE
    code_a = pltpu.roll(code_of(left, ext, right), 3 * L - start, 1)[:, 0:384]
    code_b = pltpu.roll(code_of(other(right), other(ext), other(left)), 3 * L - start, 1)[:, 0:384]

    def shifts(code):
        return [code[:, 0:L]] + [
            pltpu.roll(code, 384 - s, 1)[:, 0:L] for s in (SECOND_DILATE, 2 * SECOND_DILATE)
        ]

    three_a = shifts(code_a)
    three_b = shifts(code_b)[::-1]
    index = [jnp.concatenate([a, b], axis=1) for a, b in zip(tap_index(three_a), tap_index(three_b))]
    line = iota((ROWS, 2 * L), 0)
    hit = (line == index[0][0:1]) | (line == index[1][0:1]) | (line == index[2][0:1])
    hot_t[...] = jnp.where(hit, 1.0, 0.0).astype(BF16)
    mid_t[...] = jnp.where(
        iota((PAD, 2 * L), 0) == jnp.concatenate([three_a[1], three_b[1]], axis=1)[0:1], 1.0, 0.0
    ).astype(BF16)

    def column(row):
        return jnp.transpose(row.astype(F32))[:, 0:1].astype(jnp.int32)

    finish(p_copies)
    psum[...] = ppart[rows(y, 32)] + py[0] + py[1] + py[2]
    p_copies = [
        net.start(psum.at[rows((z + d) % 4, 8)], pz.at[z], along_z(d)) for d in range(1, 8)
    ]
    pz[z] = psum[rows(z % 4, 8)]

    columns = [column(row) for row in index]
    line = iota((2 * L, ROWS), 1)
    hit = (line == columns[0]) | (line == columns[1]) | (line == columns[2])
    hot[...] = jnp.where(hit, 1.0, 0.0).astype(BF16)
    line = iota((384, PAD), 1)
    wide_a[...] = jnp.where(line == column(code_a), 1.0, 0.0).astype(BF16)
    wide_b[...] = jnp.where(line == column(code_b), 1.0, 0.0).astype(BF16)

    finish(q_copies)
    for i in range(32):
        tile = qparts[i]
        qfull[0:8, OWN * i : OWN * i + OWN] = tile[:, 0:OWN]
        qfull[8:16, OWN * i : OWN * i + OWN] = tile[:, 64 : 64 + OWN]

    finish(p_copies)
    total = pz[0]
    for i in range(1, 8):
        total = total + pz[i]
    pmid[z % 4] = total
    p_copies = [
        net.start(pmid.at[z % 4], pmid.at[z % 4], along_half_z(d)) for d in range(1, 4)
    ]

    table_v[...] = jnp.zeros_like(table_v)
    pads = jnp.zeros((4, BLOCK), F32)
    sums = jnp.zeros((PAD, 128), F32)
    for b in range(BLOCKS):
        here = slice(BLOCK * b, BLOCK * b + BLOCK)
        pre = inv_a * dot(hot_code, qfull[:, here], HIGH)
        act, grad = gelu_parts(pre)
        center = dot(hot_code, jnp.concatenate([pads, emb[:, here], pads, pads], axis=0))
        live = iota((PAD, BLOCK), 0) < CODES
        table[:, here] = jnp.where(live, center + act, 0.0).astype(BF16)
        sv = jnp.where(live, grad * (0.5 * dot(mid_t[...], cots[:, here])), 0.0)
        table_v[:, here] = inv_a * sv
        prod = sv * pre
        sums = sums + prod[:, 0:128] + prod[:, 128:256]

    finish(p_copies)
    quarter = pl.ds(pl.multiple_of(c * 128 + y * 32, 32), 32)
    pbuf[quarter, mine] = jnp.concatenate([pmid[i] for i in range(4)], axis=0).astype(BF16)
    block = pbuf.at[quarter, mine]
    p_copies = [net.start(block, block, in_square(a, b)) for a, b in SQUARE]
    p_shares = [net.start(block, block, other_core())]

    hot_ct = code_onehot(iota((16, PAD), 1), iota((16, PAD), 0))
    fv = dot(hot_ct, table_v[...], HIGH)
    mean_v = jnp.sum(sums, axis=1, keepdims=True) * (1.0 / C)
    hot_gram = code_onehot(iota((PAD, PAD), 0), iota((PAD, PAD), 1) - 96)
    gram_v = dot(hot_ct, (inv_a * inv_a * mean_v) * hot_gram, HIGH)
    xbuf[:, C + ROWS : WIDE] = jnp.zeros((ROWS, WIDE - C - ROWS), F32)
    xbuf[0:16, C + ROWS : C + ROWS + PAD] = gram_v
    for i in range(16):
        xbuf[16 * i : 16 * i + 16, C + ROWS : C + ROWS + 96] = fv[:, 96 * i : 96 * i + 96]

    acc[...] = jnp.zeros_like(acc)
    acc2[...] = jnp.zeros_like(acc2)

    def first_pass(b, carry):
        here = lanes(b, BLOCK)
        m = table[:, here]
        taps2 = k2_ref[:, here]
        for n, (wide, order) in enumerate(((wide_a, (0, 1, 2)), (wide_b, (2, 1, 0)))):
            mid = dot(wide[...], m)
            conv = (
                taps2[order[0] : order[0] + 1] * mid[0:L]
                + taps2[order[1] : order[1] + 1] * mid[64 : 64 + L]
                + taps2[order[2] : order[2] + 1] * mid[128 : 128 + L]
            )
            square = conv * conv
            acc[n * L : n * L + L] += square[:, 0:128] + square[:, 128:256]
            mids[n * L : n * L + L, here] = mid[64 : 64 + L].astype(BF16)
        return carry

    lax.fori_loop(0, BLOCKS, first_pass, 0)
    acc[...] = jnp.broadcast_to(
        lax.rsqrt(jnp.sum(acc[...], axis=1, keepdims=True) * (1.0 / C) + EPS), (2 * L, 128)
    )

    for copy, (a, b) in zip(p_copies, SQUARE):
        copy.wait()
        here = pl.ds(pl.multiple_of(c * 128 + ((y - b + 4) % 4) * 32, 32), 32)
        block = pbuf.at[here, lanes((x - a + 4) % 4, 384)]
        p_shares.append(net.start(block, block, other_core()))
    finish(p_shares)

    base = net.take(BLOCKS)
    away = rows(1 - c, 128)

    def core_copy(b):
        here = lanes(b, BLOCK)
        return net.copy(core_send.at[:, here], from_core.at[:, here], other_core(), base + b)

    def second_pass(b, carry):
        here = lanes(b, BLOCK)
        preu[...] = dot(hot[...], pbuf[:, here])

        def chunk(r, carry):
            some = rows(r, 64)
            inv = acc[some][:, 0:1]
            pre = inv * preu[some]
            act, grad = gelu_parts(pre)
            fins[some, here] = (mids[some, here].astype(F32) + act).astype(BF16)
            sl = cots[some, here].astype(F32) * grad
            prod = sl * pre
            acc2[some] += prod[:, 0:128] + prod[:, 128:256]
            slope[some] = (inv * sl).astype(BF16)
            return carry

        lax.fori_loop(0, 8, chunk, 0)
        xbuf[:, here] = 0.5 * dot(hot_t[...], slope[...])
        core_send[:, here] = xbuf[away, here].astype(BF16)
        core_copy(b).start()
        return carry

    lax.fori_loop(0, BLOCKS, second_pass, 0)

    inv = acc[:, 0:1]
    weight = (0.5 / C) * inv * inv * jnp.sum(acc2[...], axis=1, keepdims=True)
    high, low = split(weight * hot[...].astype(F32))
    xbuf[:, C : C + ROWS] = dot(hot_t[...], high) + dot(hot_t[...], low)
    core_send[:, C:WIDE] = xbuf[away, C:WIDE].astype(BF16)
    last = net.start(core_send.at[:, C:WIDE], from_core.at[:, C:WIDE], other_core())
    for b in range(BLOCKS):
        core_copy(b).wait()
    half = rows(c, 128)
    xbuf[half, 0:C] = xbuf[half, 0:C] + from_core[:, 0:C].astype(F32)
    chip_low[:, 0:C] = xbuf[half, 0:C].astype(BF16)
    last.wait()
    xbuf[half, C:WIDE] = xbuf[half, C:WIDE] + from_core[:, C:WIDE].astype(F32)
    chip_low[:, C:WIDE] = xbuf[half, C:WIDE].astype(BF16)
    copies = []
    for j, (a, b) in enumerate(SQUARE):
        block = chip_low.at[rows((x + a) % 4, 32), lanes((y + b) % 4, QUART)]
        copies.append(net.start(block, xin.at[j], in_square(a, b)))

    def third_pass(b, carry):
        here = lanes(b, BLOCK)
        there = lanes(BLOCKS - 1 - b, BLOCK)
        far = dot(fins[L : 2 * L, there], mirror)
        out_buf[:, here] = (0.5 * (fins[0:L, here].astype(F32) + far)).astype(BF16)
        return carry

    lax.fori_loop(0, BLOCKS, third_pass, 0)
    store = pltpu.make_async_copy(out_buf, out_out, lsem.at[9])
    store.start()

    finish(copies)
    third = pl.ds(pl.multiple_of(c * 128 + x * 32, 32), 32)
    quart = lanes(y, QUART)
    total = xbuf[third, quart]
    for j in range(15):
        total = total + xin[j].astype(F32)
    xsum[0] = total[:, 0:256]
    xsum[1] = total[:, 256:512]
    copies = []
    for d in range(1, 8):
        to = (z + d) % 8
        copies.append(net.start(xsum.at[to // 4, rows(to % 4, 8)], zin.at[d - 1], along_z(d)))
    finish(copies)
    total = xsum[z // 4, rows(z % 4, 8)]
    for d in range(7):
        total = total + zin[d]
    zout[z] = total
    finish([net.start(zout.at[z], zout.at[z], along_z(d)) for d in range(1, 8)])
    for h in range(2):
        here = pl.ds(pl.multiple_of(y * QUART + h * 256, 128), 256)
        full[third, here] = jnp.concatenate([zout[4 * h + i] for i in range(4)], axis=0).astype(BF16)
    block = full.at[third, quart]
    copies = [net.start(block, block, in_square(a, b)) for a, b in SQUARE]
    shares = [net.start(block, block, other_core())]
    for copy, (a, b) in zip(copies, SQUARE):
        copy.wait()
        here = pl.ds(pl.multiple_of(c * 128 + ((x - a + 4) % 4) * 32, 32), 32)
        block = full.at[here, lanes((y - b + 4) % 4, QUART)]
        shares.append(net.start(block, block, other_core()))
    finish(shares)

    energy = full[:, 0:C]
    ew = dot_nt(energy, wpad2[...])
    high, low = split(b_own)
    gram = full[:, C : C + ROWS]
    d = g2_own * ew - (dot(gram, high) + dot(gram, low))

    def total_rows(value):
        return jnp.sum(value, axis=0, keepdims=True)

    taps_b = [
        total_rows(m_own[0:80] * d[0:80]),
        total_rows(m_own[0:96] * d[80:176]),
        total_rows(m_own[0:64] * d[176:240]) + total_rows(m_own[80:96] * d[240:256]),
    ]
    gain_b = total_rows(b_own * ew)
    up = taps[1] * d[80:176] + jnp.concatenate(
        [taps[0] * d[0:64] + taps[2] * d[176:240], taps[0] * d[64:80], taps[2] * d[240:256]],
        axis=0,
    )
    s = slope_own[0:CODES] * up
    inv = inv_a[0:CODES]
    mean_s = jnp.sum(s * pre_own[0:CODES], axis=1, keepdims=True) * (1.0 / C)
    narrow = hot_ct[:, 0:CODES]
    hot_far = code_onehot(iota((CODES, PAD), 0), iota((CODES, PAD), 1) - OWN)
    extra = C + ROWS
    fv = full[pl.ds(pl.multiple_of((pos // 2) * 16, 16), 16), extra : extra + PAD].astype(F32)
    fv = jnp.where(pos % 2 == 1, pltpu.roll(fv, PAD - OWN, 1), fv)
    fv = jnp.where(iota((16, PAD), 1) < OWN, fv, 0.0)
    own_rows = fv + dot(narrow, inv * s, HIGH)
    f_rows = jnp.where(iota((16, PAD), 0) < 12, own_rows, 0.0)
    vec_rows = jnp.concatenate([jnp.zeros((12, PAD), F32)] + taps_b + [gain_b], axis=0)
    packet = f_rows + vec_rows + dot(narrow, (inv * inv * mean_s) * hot_far, HIGH)
    pack[...] = packet[0:8] + pltpu.roll(packet[8:16], 64, 1)
    packs[pos] = pack[...]
    copies = [net.start(pack, packs.at[pos], in_plane(a, b)) for a, b in PLANE]

    high, low = split(jnp.transpose(a_own))
    both = jnp.concatenate([high[0:OWN], low[0:OWN]], axis=0)
    for b in range(0, C, 512):
        grad = dot(both, full[:, b : b + 512])
        gw_ref[OWN : 2 * OWN, b : b + 512] = grad[0:OWN] + grad[OWN : 2 * OWN]
    fbuf[...] = jnp.zeros_like(fbuf)
    finish(copies)
    total = jnp.zeros((8, PAD), F32)
    for i in range(32):
        tile = packs[i]
        fbuf[0:8, OWN * i : OWN * i + OWN] = tile[:, 0:OWN]
        fbuf[8:16, OWN * i : OWN * i + OWN] = tile[:, 64 : 64 + OWN]
        total = total + tile
    far = jnp.concatenate([total, pltpu.roll(total, 64, 1)], axis=0)
    far = far + pltpu.roll(full[0:16, extra : extra + PAD].astype(F32), PAD - OWN, 1)
    far = jnp.where((iota((16, PAD), 1) >= OWN) & (iota((16, PAD), 1) < OWN + 12), far, 0.0)
    high, low = split(fbuf[0:16])
    fw = dot_nt(jnp.concatenate([high, low], axis=0), wpad1[...])
    fw = fw[0:16] + fw[16:32]
    spread = jnp.concatenate(
        [jnp.zeros((OWN, PAD), F32), te_own, jnp.zeros((64, PAD), F32)], axis=0
    )
    da = g1_own * fw - dot(far, spread, HIGH)
    rows_a = [total_rows(e_own * da[4 * k : 4 * k + 4]) for k in range(3)]
    rows_a = rows_a + [total_rows(te_own * fw)]
    pack2[...] = jnp.concatenate(
        [
            rows_a[0] + pltpu.roll(rows_a[1], 64, 1),
            rows_a[2] + pltpu.roll(rows_a[3], 64, 1),
        ],
        axis=0,
    )
    packs2[pos] = pack2[...]
    copies = [net.start(pack2, packs2.at[pos], in_plane(a, b)) for a, b in PLANE]

    wide = jnp.concatenate([g1_own * te_own, jnp.zeros((PAD - 16, PAD), F32)], axis=0)
    wide = jnp.transpose(wide)
    for b in range(0, C, 512):
        gw_ref[0:OWN, b : b + 512] = dot(wide, fbuf[:, b : b + 512], HIGH)[0:OWN]
    vec_ref[4:8, :] = fbuf[12:16, :]
    finish(copies)
    for i in range(32):
        tile = packs2[i]
        here = slice(OWN * i, OWN * i + OWN)
        vec_ref[0:1, here] = tile[0:1, 0:OWN]
        vec_ref[1:2, here] = tile[0:1, 64 : 64 + OWN]
        vec_ref[2:3, here] = tile[1:2, 0:OWN]
        vec_ref[3:4, here] = tile[1:2, 64 : 64 + OWN]
    store.wait()


def whole(*args):
    vmem = pl.BlockSpec(memory_space=pltpu.VMEM)
    hbm = pl.BlockSpec(memory_space=pl.ANY)
    return pl.pallas_call(
        whole_kernel,
        out_shape=(
            jax.ShapeDtypeStruct((L, C), BF16),
            jax.ShapeDtypeStruct((2 * OWN, C), F32),
            jax.ShapeDtypeStruct((8, C), F32),
        ),
        in_specs=[hbm] * 9,
        out_specs=(hbm, vmem, vmem),
        scratch_shapes=[
            pltpu.VMEM((1, L), jnp.int32),
            pltpu.VMEM((4, C), BF16),
            pltpu.VMEM((3, C), F32),
            pltpu.VMEM((1, C), F32),
            pltpu.VMEM((3, C), F32),
            pltpu.VMEM((1, C), F32),
            pltpu.VMEM((PAD, C), BF16),
            pltpu.VMEM((PAD, C), BF16),
            pltpu.VMEM((L, C), BF16),
            pltpu.VMEM((8, L), jnp.int32),
            pltpu.VMEM((3, 8, L), jnp.int32),
            pltpu.VMEM((32, 8, PAD), F32),
            pltpu.VMEM((32, 8, PAD), F32),
            pltpu.VMEM((8, PAD), F32),
            pltpu.VMEM((32, 8, PAD), F32),
            pltpu.VMEM((16, C), F32),
            pltpu.VMEM((ROWS, PAD), F32),
            pltpu.VMEM((128, 384), F32),
            pltpu.VMEM((3, 32, 384), F32),
            pltpu.VMEM((32, 384), F32),
            pltpu.VMEM((8, 8, 384), F32),
            pltpu.VMEM((4, 8, 384), F32),
            pltpu.VMEM((ROWS, C), BF16),
            pltpu.VMEM((PAD, C), BF16),
            pltpu.VMEM((8, PAD), F32),
            pltpu.VMEM((PAD, C), F32),
            pltpu.VMEM((2 * L, ROWS), BF16),
            pltpu.VMEM((ROWS, 2 * L), BF16),
            pltpu.VMEM((384, PAD), BF16),
            pltpu.VMEM((384, PAD), BF16),
            pltpu.VMEM((PAD, 2 * L), BF16),
            pltpu.VMEM((2 * L, C), BF16),
            pltpu.VMEM((2 * L, C), BF16),
            pltpu.VMEM((2 * L, C), BF16),
            pltpu.VMEM((2 * L, BLOCK), F32),
            pltpu.VMEM((2 * L, BLOCK), BF16),
            pltpu.VMEM((2 * L, 128), F32),
            pltpu.VMEM((2 * L, 128), F32),
            pltpu.VMEM((L, C), BF16),
            pltpu.VMEM((ROWS, WIDE), F32),
            pltpu.VMEM((128, WIDE), BF16),
            pltpu.VMEM((128, WIDE), BF16),
            pltpu.VMEM((128, WIDE), BF16),
            pltpu.VMEM((15, 32, QUART), BF16),
            pltpu.VMEM((2, 32, 256), F32),
            pltpu.VMEM((7, 8, 256), F32),
            pltpu.VMEM((8, 8, 256), F32),
            pltpu.VMEM((ROWS, WIDE), BF16),
            pltpu.VMEM((8, PAD), F32),
            pltpu.VMEM((32, 8, PAD), F32),
            pltpu.VMEM((PAD, C), F32),
            pltpu.VMEM((2, PAD), F32),
            pltpu.VMEM((32, 2, PAD), F32),
            pltpu.SemaphoreType.DMA((10,)),
            pltpu.SemaphoreType.DMA((2, 3)),
            pltpu.SemaphoreType.DMA((256,)),
            pltpu.SemaphoreType.DMA((256,)),
        ],
        compiler_params=pltpu.CompilerParams(
            collective_id=0, has_side_effects=True, vmem_limit_bytes=62 * 2**20
        ),
        name="whole",
    )(*args)


def shards(tokens, embed, k1, g1, w1, k2, g2, w2, cotangent):
    out, gw, vec = whole(
        tokens,
        embed,
        k1,
        g1.reshape(1, C),
        w1,
        k2,
        g2.reshape(1, C),
        w2,
        cotangent.reshape(L, C),
    )
    return (
        out[None, None],
        gw[0:OWN],
        gw[OWN:],
        vec[0:3],
        vec[4:7],
        vec[3],
        vec[7],
    )


def solution(mesh):
    placed = (
        P("rep", "pos"),
        P(),
        P(),
        P(),
        P("pos", None),
        P(),
        P(),
        P("pos", None),
        P("rep", "strand", "pos", None),
    )
    return jax.shard_map(
        shards,
        mesh=mesh,
        in_specs=placed,
        out_specs=(
            P("rep", "strand", "pos", None),
            P("pos", None),
            P("pos", None),
            P(),
            P(),
            P(),
            P(),
        ),
        check_vma=False,
    )
```

time: 1040 us -> 110 us (0.11)
  waiting for transfers between devices: 789 us -> 0 us
  blocking collectives: 118 us -> 0 us
  Pallas kernels: 0 us -> 101 us
  matrix products: 37.6 us -> 0 us
  local copies, waits for them, and re-layouts: 36 us -> 7.71 us
  starting transfers between devices: 25.4 us -> 0 us
  other arithmetic: 15.7 us -> 0 us
  between operations: 14.3 us -> 0.66 us
    reduce_scatter x2 -> x0, waiting for transfers between devices: 411 us -> none  [weight_grad(): lax.psum_scatter(lax.dot_general(normed, slopes, (((0,), (0,)), ((), ()))...]
    ppermute x12 -> x0, waiting for transfers between devices: 271 us -> none  [the longest x6 264 us: swapped(): return lax.ppermute(value, axis, pairs)]
    all_gather x2 -> x0, waiting for transfers between devices: 106 us -> none  [the longest x1 67.3 us: shards(): lax.all_gather(second_weight, 'pos', axis=0, tiled=True)]
    pallas_call x0 -> x1, Pallas kernels: none -> 101 us  [whole(): pl.pallas_call(whole_kernel, out_shape=(jax.ShapeDtypeStruct((L, C), BF16...]
    psum x1 -> x0, blocking collectives: 79.5 us -> none  [shards(): lax.psum((first_kernel_share, first_gain_share, second_kernel_share, seco...]
    all_gather x1 -> x0, blocking collectives: 38.4 us -> none  [shards(): whole_tokens = lax.all_gather(own_tokens, 'pos', axis=0, tiled=True)]
    dot_general x7 -> x0, matrix products: 37.6 us -> none  [the longest x2 13.2 us: weight_grad(): lax.dot_general(normed, slopes, (((0,), (0,)), ((), ())), preferred_eleme...]
    rev x3 -> x0, local copies, waits for them, and re-layouts: 25.3 us -> none  [the longest x1 12.6 us: shards(): cot_far[::-1, ::-1].astype(jnp.float32)]
  transfers between devices with their start and end apart: 17 -> 0, of which waited for: 16 -> 0; matrix products, arithmetic and copies ran while one was open for 5% -> 0% of each run, Pallas kernels for 0% -> 0%
where the time goes in v2:
time: 110 us; the launch traced here: 109 us
  Pallas kernels  101 us (92%)
  local copies, waits for them, and re-layouts  7.71 us (7%)
    pallas_call x1, Pallas kernels, whole(): pl.pallas_call(whole_kernel, out_shape=(jax.ShapeDtypeStruct((L, C), BF16...  101 us

profile of v2, /device:TPU:1, one launch (start us, length us, event | category | flops | bytes accessed | tf_op | source)
XLA Modules:
  0.0 109.4 jit_solution(10480625485443055373)
XLA Ops:
  0.6 0.0 copy-start.1
  0.6 1.3 %reshape.23.g1_in = f32[1,1536]{1,0:T(1,128)} reshape(f32[1536]{0:T(1024)} %param.12) | data formatting | bytes 12288 | tf_op jit(solution)/shard_map/reshape | solution.py:777
  1.9 0.0 copy-done.1
  1.9 0.6 reshape.24.g2_in
  2.5 101.0 %whole.1 = (bf16[256,1536]{1,0:T(8,128)(2,1)}, f32[96,1536]{1,0:T(8,128)}, f32[8,1536]{1,0:T(8,128)}) custom-call(s32[1,256]{1,0:T(1,128)} %tok_in.1, bf16[4,1536]{1,0:T(4,128)(2,1)} %emb_in.1, f32[3,1536]{1,0:T(4,128)} %k1_in.1, f32[1,1536]{1,0:T(1,128)} %reshape.23.g1_in, bf16[48,1536]{1,0:T(8,128)(2,1)} %w1_in.1, f32[3,1536]{1,0:T(4,128)} %k2_in.1, ...), custom_call_target="tpu_custom_call" | custom-call | tf_op jit(solution)/shard_map/whole/pallas_call | solution.py:697
  103.6 0.0 copy-start
  103.6 1.5 %slice_reduce_fusion = (f32[1536]{0:T(1024)}, f32[1536]{0:T(1024)}) fusion(f32[8,1536]{1,0:T(8,128)} %get-tuple-element.12), kind=kLoop, calls=%fused_computation | loop fusion | bytes 24576 | tf_op jit(solution)/shard_map/slice | solution.py:791
  105.1 1.5 %fusion.1 = (f32[3,1536]{1,0:T(4,128)}, f32[3,1536]{1,0:T(4,128)}) fusion(f32[8,1536]{1,0:T(8,128)} %get-tuple-element.12), kind=kLoop, calls=%fused_computation.3 | loop fusion | bytes 73728 | tf_op jit(solution)/shard_map/slice | solution.py:789
  106.6 1.9 %fusion = (f32[48,1536]{1,0:T(8,128)}, f32[48,1536]{1,0:T(8,128)}) fusion(f32[96,1536]{1,0:T(8,128)} %get-tuple-element.11), kind=kLoop, calls=%fused_computation.2 | loop fusion | bytes 1179648 | tf_op jit(solution)/shard_map/slice | solution.py:787
  108.5 0.0 copy-done
  108.5 0.9 copy.17
Async XLA Ops:
  0.6 1.3 %copy-start.1 = (f32[1536]{0:T(1024)S(1)}, f32[1536]{0:T(1024)}, u32[]{:S(2)}) copy-start(f32[1536]{0:T(1024)} %param.15) | copy-start | bytes 18436
  103.6 4.9 %copy-start = (bf16[256,1536]{1,0:T(8,128)(2,1)S(1)}, bf16[256,1536]{1,0:T(8,128)(2,1)}, u32[]{:S(2)}) copy-start(bf16[256,1536]{1,0:T(8,128)(2,1)} %get-tuple-element.10) | copy-start | bytes 2359300

commit v3 on v2

--- a/solution.py
+++ b/solution.py
@@ -20,7 +20,6 @@
 PAD = 128
 ROWS = 256
 WIDE = 2048
-QUART = WIDE // 4
 BLOCK = 256
 BLOCKS = C // BLOCK
 OWN = 48
@@ -128,10 +127,10 @@
 
 def gelu_parts(pre):
     square = pre * pre
-    th = jnp.tanh(GELU_A * pre * (1.0 + GELU_B * square))
-    half = 0.5 * (1.0 + th)
-    slope = half + 0.5 * pre * (1.0 - th * th) * (GELU_A * (1.0 + 3.0 * GELU_B * square))
-    return pre * half, slope
+    th = jnp.tanh(pre * (GELU_A + (GELU_A * GELU_B) * square))
+    half = 0.5 + 0.5 * th
+    bend = pre * (GELU_A + (3.0 * GELU_A * GELU_B) * square)
+    return pre * half, half * (1.0 + (1.0 - th) * bend)
 
 
 def code_bases(code):
@@ -285,15 +284,11 @@
     for peer in peers:
         pl.semaphore_signal(barrier, inc=1, device_id=peer, device_id_type=MESH)
 
-    for load in loads[:7]:
+    for load in loads[:6]:
         load.wait()
-    tokens = jnp.broadcast_to(tok[...], (8, L)).astype(F32)
-    flip = jnp.where(iota((L, L), 0) + iota((L, L), 1) == L - 1, 1.0, 0.0)
-    turned = 3.0 - dot(tokens, flip)
-    tsend[...] = jnp.where(strand == 1, turned, tokens).astype(jnp.int32)
     emb = emb16[...].astype(F32)
     k1, k2 = k1_ref[...], k2_ref[...]
-    g1, g2 = g1_ref[...], g2_ref[...]
+    g1, g2 = g1_ref[...].reshape(1, C), g2_ref[...].reshape(1, C)
     packed = jnp.concatenate([emb, k1, g1, k2, g2, jnp.zeros((4, C), F32)], axis=0)
     vec = pltpu.roll(packed, lax.rem(C - pos * OWN, C), 1)[:, 0:PAD]
     vec = jnp.where(iota((16, PAD), 1) < OWN, vec, 0.0)
@@ -312,6 +307,17 @@
     qrecv[pos] = qsend[pos]
 
     pl.semaphore_wait(barrier, len(peers))
+
+    q_copies = []
+    for a, b in PLANE:
+        there = ((y + a) % 4) * 8 + (z + b) % 8
+        q_copies.append(net.start(qsend.at[there], qrecv.at[pos], in_plane(a, b)))
+
+    loads[6].wait()
+    tokens = jnp.broadcast_to(tok[...], (8, L)).astype(F32)
+    flip = jnp.where(iota((L, L), 0) + iota((L, L), 1) == L - 1, 1.0, 0.0)
+    turned = 3.0 - dot(tokens, flip)
+    tsend[...] = jnp.where(strand == 1, turned, tokens).astype(jnp.int32)
 
     def token_copy(j):
         return pltpu.make_async_remote_copy(
@@ -332,11 +338,6 @@
         def _():
             trecv[2 - j] = tsend[...]
 
-    q_copies = []
-    for a, b in PLANE:
-        there = ((y + a) % 4) * 8 + (z + b) % 8
-        q_copies.append(net.start(qsend.at[there], qrecv.at[pos], in_plane(a, b)))
-
     te = jnp.concatenate([k1[k : k + 1] * emb for k in range(3)] + [jnp.zeros((4, C), F32)], axis=0)
     hot_code = code_onehot(iota((PAD, 16), 0), iota((PAD, 16), 1))
     conv = dot(hot_code, te, HIGH)
@@ -363,7 +364,6 @@
         total = total + qrecv[i]
     qown[...] = total
     qparts[pos] = total
-    q_copies = [net.start(qown, qparts.at[pos], in_plane(a, b)) for a, b in PLANE]
 
     q_two = jnp.concatenate([total, pltpu.roll(total, 64, 1)], axis=0)
     q_two = jnp.where(iota((16, PAD), 1) < OWN, q_two, 0.0)
@@ -383,6 +383,7 @@
     p_copies = [
         net.start(ppart.at[rows((y + d) % 4, 32)], py.at[d - 1], along_y(d)) for d in range(1, 4)
     ]
+    q_copies = [net.start(qown, qparts.at[pos], in_plane(a, b)) for a, b in PLANE]
 
     for j in range(3):
         @pl.when(targets[j] != pos)
@@ -440,19 +441,19 @@
         qfull[0:8, OWN * i : OWN * i + OWN] = tile[:, 0:OWN]
         qfull[8:16, OWN * i : OWN * i + OWN] = tile[:, 64 : 64 + OWN]
 
-    finish(p_copies)
-    total = pz[0]
-    for i in range(1, 8):
-        total = total + pz[i]
-    pmid[z % 4] = total
-    p_copies = [
-        net.start(pmid.at[z % 4], pmid.at[z % 4], along_half_z(d)) for d in range(1, 4)
-    ]
-
     table_v[...] = jnp.zeros_like(table_v)
     pads = jnp.zeros((4, BLOCK), F32)
     sums = jnp.zeros((PAD, 128), F32)
     for b in range(BLOCKS):
+        if b == BLOCKS // 2:
+            finish(p_copies)
+            total = pz[0]
+            for i in range(1, 8):
+                total = total + pz[i]
+            pmid[z % 4] = total
+            p_copies = [
+                net.start(pmid.at[z % 4], pmid.at[z % 4], along_half_z(d)) for d in range(1, 4)
+            ]
         here = slice(BLOCK * b, BLOCK * b + BLOCK)
         pre = inv_a * dot(hot_code, qfull[:, here], HIGH)
         act, grad = gelu_parts(pre)
@@ -525,14 +526,17 @@
 
         def chunk(r, carry):
             some = rows(r, 64)
-            inv = acc[some][:, 0:1]
-            pre = inv * preu[some]
-            act, grad = gelu_parts(pre)
-            fins[some, here] = (mids[some, here].astype(F32) + act).astype(BF16)
-            sl = cots[some, here].astype(F32) * grad
-            prod = sl * pre
-            acc2[some] += prod[:, 0:128] + prod[:, 128:256]
-            slope[some] = (inv * sl).astype(BF16)
+            inv = acc[some]
+            kept = acc2[some]
+            for part in (0, 128):
+                cut = pl.ds(pl.multiple_of(b * BLOCK + part, 128), 128)
+                pre = inv * preu[some, part : part + 128]
+                act, grad = gelu_parts(pre)
+                fins[some, cut] = (mids[some, cut].astype(F32) + act).astype(BF16)
+                sl = cots[some, cut].astype(F32) * grad
+                kept = kept + sl * pre
+                slope[some, part : part + 128] = (inv * sl).astype(BF16)
+            acc2[some] = kept
             return carry
 
         lax.fori_loop(0, 8, chunk, 0)
@@ -541,7 +545,69 @@
         core_copy(b).start()
         return carry
 
-    lax.fori_loop(0, BLOCKS, second_pass, 0)
+    half = rows(c, 128)
+    third = pl.ds(pl.multiple_of(c * 128 + x * 32, 32), 32)
+
+    def chip_sum(first, last):
+        xbuf[half, first:last] = xbuf[half, first:last] + from_core[:, first:last].astype(F32)
+        chip_low[:, first:last] = xbuf[half, first:last].astype(BF16)
+
+    def strip(h, at):
+        return pl.ds(pl.multiple_of(1024 * h + at * 256, 128), 256)
+
+    def square_scatter(h):
+        return [
+            net.start(
+                chip_low.at[rows((x + a) % 4, 32), strip(h, (y + b) % 4)], xin.at[h, j], in_square(a, b)
+            )
+            for j, (a, b) in enumerate(SQUARE)
+        ]
+
+    def line_scatter(h, copies):
+        finish(copies)
+        total = xbuf[third, strip(h, y)]
+        for j in range(15):
+            total = total + xin[h, j].astype(F32)
+        xsum[h, 0] = total[:, 0:128]
+        xsum[h, 1] = total[:, 128:256]
+        started = []
+        for d in range(1, 8):
+            to = (z + d) % 8
+            block = xsum.at[h, to // 4, rows(to % 4, 8)]
+            started.append(net.start(block, zin.at[h, d - 1], along_z(d)))
+        return started
+
+    def line_gather(h, copies):
+        finish(copies)
+        total = xsum[h, z // 4, rows(z % 4, 8)]
+        for d in range(7):
+            total = total + zin[h, d]
+        zout[h, z] = total
+        return [net.start(zout.at[h, z], zout.at[h, z], along_z(d)) for d in range(1, 8)]
+
+    def square_gather(h, copies):
+        finish(copies)
+        for i in range(2):
+            here = pl.ds(pl.multiple_of(1024 * h + y * 256 + 128 * i, 128), 128)
+            tiles = [zout[h, 4 * i + q] for q in range(4)]
+            full[third, here] = jnp.concatenate(tiles, axis=0).astype(BF16)
+        block = full.at[third, strip(h, y)]
+        shares = [net.start(block, block, other_core())]
+        return [net.start(block, block, in_square(a, b)) for a, b in SQUARE], shares
+
+    def share(h, copies, shares):
+        for copy, (a, b) in zip(copies, SQUARE):
+            copy.wait()
+            here = pl.ds(pl.multiple_of(c * 128 + ((x - a + 4) % 4) * 32, 32), 32)
+            block = full.at[here, strip(h, (y - b + 4) % 4)]
+            shares.append(net.start(block, block, other_core()))
+
+    lax.fori_loop(0, 4, second_pass, 0)
+    for b in range(4):
+        core_copy(b).wait()
+    chip_sum(0, 1024)
+    scatter_0 = square_scatter(0)
+    lax.fori_loop(4, BLOCKS, second_pass, 0)
 
     inv = acc[:, 0:1]
     weight = (0.5 / C) * inv * inv * jnp.sum(acc2[...], axis=1, keepdims=True)
@@ -549,18 +615,13 @@
     xbuf[:, C : C + ROWS] = dot(hot_t[...], high) + dot(hot_t[...], low)
     core_send[:, C:WIDE] = xbuf[away, C:WIDE].astype(BF16)
     last = net.start(core_send.at[:, C:WIDE], from_core.at[:, C:WIDE], other_core())
-    for b in range(BLOCKS):
+    for b in range(4, BLOCKS):
         core_copy(b).wait()
-    half = rows(c, 128)
-    xbuf[half, 0:C] = xbuf[half, 0:C] + from_core[:, 0:C].astype(F32)
-    chip_low[:, 0:C] = xbuf[half, 0:C].astype(BF16)
+    chip_sum(1024, C)
     last.wait()
-    xbuf[half, C:WIDE] = xbuf[half, C:WIDE] + from_core[:, C:WIDE].astype(F32)
-    chip_low[:, C:WIDE] = xbuf[half, C:WIDE].astype(BF16)
-    copies = []
-    for j, (a, b) in enumerate(SQUARE):
-        block = chip_low.at[rows((x + a) % 4, 32), lanes((y + b) % 4, QUART)]
-        copies.append(net.start(block, xin.at[j], in_square(a, b)))
+    chip_sum(C, WIDE)
+    scatter_1 = square_scatter(1)
+    line_0 = line_scatter(0, scatter_0)
 
     def third_pass(b, carry):
         here = lanes(b, BLOCK)
@@ -573,39 +634,28 @@
     store = pltpu.make_async_copy(out_buf, out_out, lsem.at[9])
     store.start()
 
-    finish(copies)
-    third = pl.ds(pl.multiple_of(c * 128 + x * 32, 32), 32)
-    quart = lanes(y, QUART)
-    total = xbuf[third, quart]
-    for j in range(15):
-        total = total + xin[j].astype(F32)
-    xsum[0] = total[:, 0:256]
-    xsum[1] = total[:, 256:512]
-    copies = []
-    for d in range(1, 8):
-        to = (z + d) % 8
-        copies.append(net.start(xsum.at[to // 4, rows(to % 4, 8)], zin.at[d - 1], along_z(d)))
-    finish(copies)
-    total = xsum[z // 4, rows(z % 4, 8)]
-    for d in range(7):
-        total = total + zin[d]
-    zout[z] = total
-    finish([net.start(zout.at[z], zout.at[z], along_z(d)) for d in range(1, 8)])
-    for h in range(2):
-        here = pl.ds(pl.multiple_of(y * QUART + h * 256, 128), 256)
-        full[third, here] = jnp.concatenate([zout[4 * h + i] for i in range(4)], axis=0).astype(BF16)
-    block = full.at[third, quart]
-    copies = [net.start(block, block, in_square(a, b)) for a, b in SQUARE]
-    shares = [net.start(block, block, other_core())]
-    for copy, (a, b) in zip(copies, SQUARE):
-        copy.wait()
-        here = pl.ds(pl.multiple_of(c * 128 + ((x - a + 4) % 4) * 32, 32), 32)
-        block = full.at[here, lanes((y - b + 4) % 4, QUART)]
-        shares.append(net.start(block, block, other_core()))
-    finish(shares)
-
-    energy = full[:, 0:C]
-    ew = dot_nt(energy, wpad2[...])
+    gather_0 = line_gather(0, line_0)
+    line_1 = line_scatter(1, scatter_1)
+    back_0, shares_0 = square_gather(0, gather_0)
+    gather_1 = line_gather(1, line_1)
+    back_1, shares_1 = square_gather(1, gather_1)
+    share(0, back_0, shares_0)
+    finish(shares_0)
+    turned_high, turned_low = split(jnp.transpose(a_own))
+    both = jnp.concatenate([turned_high[0:OWN], turned_low[0:OWN]], axis=0)
+
+    def grad_b(b):
+        grad = dot(both, full[:, b : b + 512])
+        gw_ref[OWN : 2 * OWN, b : b + 512] = grad[0:OWN] + grad[OWN : 2 * OWN]
+
+    ew = dot_nt(full[:, 0:1024], wpad2[:, 0:1024])
+    grad_b(0)
+    grad_b(512)
+    fbuf[...] = jnp.zeros_like(fbuf)
+    share(1, back_1, shares_1)
+    finish(shares_1)
+
+    ew = ew + dot_nt(full[:, 1024:C], wpad2[:, 1024:C])
     high, low = split(b_own)
     gram = full[:, C : C + ROWS]
     d = g2_own * ew - (dot(gram, high) + dot(gram, low))
@@ -640,12 +690,7 @@
     packs[pos] = pack[...]
     copies = [net.start(pack, packs.at[pos], in_plane(a, b)) for a, b in PLANE]
 
-    high, low = split(jnp.transpose(a_own))
-    both = jnp.concatenate([high[0:OWN], low[0:OWN]], axis=0)
-    for b in range(0, C, 512):
-        grad = dot(both, full[:, b : b + 512])
-        gw_ref[OWN : 2 * OWN, b : b + 512] = grad[0:OWN] + grad[OWN : 2 * OWN]
-    fbuf[...] = jnp.zeros_like(fbuf)
+    grad_b(1024)
     finish(copies)
     total = jnp.zeros((8, PAD), F32)
     for i in range(32):
@@ -693,7 +738,8 @@
 
 def whole(*args):
     vmem = pl.BlockSpec(memory_space=pltpu.VMEM)
-    hbm = pl.BlockSpec(memory_space=pl.ANY)
+    hbm = pl.BlockSpec(memory_space=pltpu.HBM)
+    anywhere = pl.BlockSpec(memory_space=pl.ANY)
     return pl.pallas_call(
         whole_kernel,
         out_shape=(
@@ -702,14 +748,14 @@
             jax.ShapeDtypeStruct((8, C), F32),
         ),
         in_specs=[hbm] * 9,
-        out_specs=(hbm, vmem, vmem),
+        out_specs=(anywhere, vmem, vmem),
         scratch_shapes=[
             pltpu.VMEM((1, L), jnp.int32),
             pltpu.VMEM((4, C), BF16),
             pltpu.VMEM((3, C), F32),
-            pltpu.VMEM((1, C), F32),
+            pltpu.VMEM((C,), F32),
             pltpu.VMEM((3, C), F32),
-            pltpu.VMEM((1, C), F32),
+            pltpu.VMEM((C,), F32),
             pltpu.VMEM((PAD, C), BF16),
             pltpu.VMEM((PAD, C), BF16),
             pltpu.VMEM((L, C), BF16),
@@ -747,10 +793,10 @@
             pltpu.VMEM((128, WIDE), BF16),
             pltpu.VMEM((128, WIDE), BF16),
             pltpu.VMEM((128, WIDE), BF16),
-            pltpu.VMEM((15, 32, QUART), BF16),
-            pltpu.VMEM((2, 32, 256), F32),
-            pltpu.VMEM((7, 8, 256), F32),
-            pltpu.VMEM((8, 8, 256), F32),
+            pltpu.VMEM((2, 15, 32, 256), BF16),
+            pltpu.VMEM((2, 2, 32, 128), F32),
+            pltpu.VMEM((2, 7, 8, 128), F32),
+            pltpu.VMEM((2, 8, 8, 128), F32),
             pltpu.VMEM((ROWS, WIDE), BF16),
             pltpu.VMEM((8, PAD), F32),
             pltpu.VMEM((32, 8, PAD), F32),
@@ -759,8 +805,8 @@
             pltpu.VMEM((32, 2, PAD), F32),
             pltpu.SemaphoreType.DMA((10,)),
             pltpu.SemaphoreType.DMA((2, 3)),
-            pltpu.SemaphoreType.DMA((256,)),
-            pltpu.SemaphoreType.DMA((256,)),
+            pltpu.SemaphoreType.DMA((320,)),
+            pltpu.SemaphoreType.DMA((320,)),
         ],
         compiler_params=pltpu.CompilerParams(
             collective_id=0, has_side_effects=True, vmem_limit_bytes=62 * 2**20
@@ -769,27 +815,40 @@
     )(*args)
 
 
+def place_kernel(out_in, gw_in, vec_ref, out_ref, gwa_ref, gwb_ref, ta_ref, tb_ref, ga_ref, gb_ref):
+    out_ref[...] = out_in[...]
+    gwa_ref[...] = gw_in[0:OWN]
+    gwb_ref[...] = gw_in[OWN : 2 * OWN]
+    ta_ref[...] = vec_ref[0:3]
+    tb_ref[...] = vec_ref[4:7]
+    ga_ref[...] = vec_ref[3]
+    gb_ref[...] = vec_ref[7]
+
+
+def placed_outputs(out, gw, vec):
+    vmem = pl.BlockSpec(memory_space=pltpu.VMEM)
+    return pl.pallas_call(
+        place_kernel,
+        out_shape=(
+            jax.ShapeDtypeStruct((L, C), BF16),
+            jax.ShapeDtypeStruct((OWN, C), F32),
+            jax.ShapeDtypeStruct((OWN, C), F32),
+            jax.ShapeDtypeStruct((3, C), F32),
+            jax.ShapeDtypeStruct((3, C), F32),
+            jax.ShapeDtypeStruct((C,), F32),
+            jax.ShapeDtypeStruct((C,), F32),
+        ),
+        in_specs=[vmem] * 3,
+        out_specs=(vmem,) * 7,
+        compiler_params=pltpu.CompilerParams(vmem_limit_bytes=62 * 2**20),
+        name="place",
+    )(out, gw, vec)
+
+
 def shards(tokens, embed, k1, g1, w1, k2, g2, w2, cotangent):
-    out, gw, vec = whole(
-        tokens,
-        embed,
-        k1,
-        g1.reshape(1, C),
-        w1,
-        k2,
-        g2.reshape(1, C),
-        w2,
-        cotangent.reshape(L, C),
-    )
-    return (
-        out[None, None],
-        gw[0:OWN],
-        gw[OWN:],
-        vec[0:3],
-        vec[4:7],
-        vec[3],
-        vec[7],
-    )
+    out, gw, vec = whole(tokens, embed, k1, g1, w1, k2, g2, w2, cotangent.reshape(L, C))
+    out, gwa, gwb, ta, tb, ga, gb = placed_outputs(out, gw, vec)
+    return (out[None, None], gwa, gwb, ta, tb, ga, gb)
 
 
 def solution(mesh):

time: 110 us -> 99 us (0.900)
  local copies, waits for them, and re-layouts: 7.71 us -> 0 us
  Pallas kernels: 101 us -> 98.2 us
    pallas_call x1, Pallas kernels: 101 us -> 95.7 us  [whole(): pl.pallas_call(whole_kernel, out_shape=(jax.ShapeDtypeStruct((L, C), BF16...]
    slice x3 -> x0, local copies, waits for them, and re-layouts: 4.93 us -> none  [the longest x1 1.9 us: shards(): gw[OWN:]]
    pallas_call x0 -> x1, Pallas kernels: none -> 2.43 us  [placed_outputs(): pl.pallas_call(place_kernel, out_shape=(jax.ShapeDtypeStruct((L, C), BF16...]
    reshape x2 -> x0, local copies, waits for them, and re-layouts: 1.9 us -> none  [the longest x1 1.3 us: shards(): g1.reshape(1, C)]
where the time goes in v3:
time: 99 us; the launch traced here: 98.8 us
  Pallas kernels  98.2 us (99%)
    pallas_call x1, Pallas kernels, whole(): pl.pallas_call(whole_kernel, out_shape=(jax.ShapeDtypeStruct((L, C), BF16...  95.7 us
    pallas_call x1, Pallas kernels, placed_outputs(): pl.pallas_call(place_kernel, out_shape=(jax.ShapeDtypeStruct((L, C), BF16...  2.43 us

profile of v3, /device:TPU:1, one launch (start us, length us, event | category | flops | bytes accessed | tf_op | source)
XLA Modules:
  0.0 98.8 jit_solution(11891901510778280908)
XLA Ops:
  0.6 95.7 %whole.1 = (bf16[256,1536]{1,0:T(8,128)(2,1)}, f32[96,1536]{1,0:T(8,128)}, f32[8,1536]{1,0:T(8,128)}) custom-call(s32[1,256]{1,0:T(1,128)} %tok_in.1, bf16[4,1536]{1,0:T(4,128)(2,1)} %emb_in.1, f32[3,1536]{1,0:T(4,128)} %k1_in.1, f32[1536]{0:T(1024)} %g1_in.1, bf16[48,1536]{1,0:T(8,128)(2,1)} %w1_in.1, f32[3,1536]{1,0:T(4,128)} %k2_in.1, f32[1536]{0:T(1024)} %g2_in.1, ...), custom_call_target="tpu_custom_call" | custom-call | tf_op jit(solution)/shard_map/whole/pallas_call | solution.py:743
  96.4 2.4 %place.1 = (bf16[256,1536]{1,0:T(8,128)(2,1)}, f32[48,1536]{1,0:T(8,128)}, f32[48,1536]{1,0:T(8,128)}, f32[3,1536]{1,0:T(4,128)}, f32[3,1536]{1,0:T(4,128)}, /*index=5*/f32[1536]{0:T(1024)}, f32[1536]{0:T(1024)}) custom-call(bf16[256,1536]{1,0:T(8,128)(2,1)} %get-tuple-element.17.out_in, f32[96,1536]{1,0:T(8,128)} %get-tuple-element.18.gw_in, ...), custom_call_target="tpu_custom_call" | custom-call | tf_op jit(solution)/shard_map/place/pallas_call | solution.py:830

commit v4 on v3

--- a/solution.py
+++ b/solution.py
@@ -91,15 +91,21 @@
             device_id_type=MESH,
         )
 
-    def start(self, src, dst, to):
-        copy = self.copy(src, dst, to, self.take(1))
-        copy.start()
-        return copy
-
-
-def finish(copies):
-    for copy in copies:
-        copy.wait()
+    def start(self, items, total):
+        sem = self.take(1)
+        for src, dst, to in items:
+            self.copy(src, dst, to, sem).start()
+        return self.copy(total, total, other_core(), sem)
+
+
+def share_out(onehot, value, parts):
+    total = None
+    for _ in range(parts):
+        part = value.astype(BF16)
+        value = value - part.astype(F32)
+        term = dot(onehot.astype(BF16), part)
+        total = term if total is None else total + term
+    return total
 
 
 def lanes(index, width):
@@ -308,10 +314,13 @@
 
     pl.semaphore_wait(barrier, len(peers))
 
-    q_copies = []
-    for a, b in PLANE:
-        there = ((y + a) % 4) * 8 + (z + b) % 8
-        q_copies.append(net.start(qsend.at[there], qrecv.at[pos], in_plane(a, b)))
+    q_copies = net.start(
+        [
+            (qsend.at[((y + a) % 4) * 8 + (z + b) % 8], qrecv.at[pos], in_plane(a, b))
+            for a, b in PLANE
+        ],
+        qrecv.at[0:31],
+    )
 
     loads[6].wait()
     tokens = jnp.broadcast_to(tok[...], (8, L)).astype(F32)
@@ -340,7 +349,7 @@
 
     te = jnp.concatenate([k1[k : k + 1] * emb for k in range(3)] + [jnp.zeros((4, C), F32)], axis=0)
     hot_code = code_onehot(iota((PAD, 16), 0), iota((PAD, 16), 1))
-    conv = dot(hot_code, te, HIGH)
+    conv = share_out(hot_code, te, 3)
     inv_a = lax.rsqrt(jnp.mean(conv * conv, axis=-1, keepdims=True) + EPS)
 
     mirror = jnp.where(
@@ -358,7 +367,7 @@
 
     lax.fori_loop(0, BLOCKS, turn_cot, 0)
 
-    finish(q_copies)
+    q_copies.wait()
     total = qrecv[0]
     for i in range(1, 32):
         total = total + qrecv[i]
@@ -367,10 +376,10 @@
 
     q_two = jnp.concatenate([total, pltpu.roll(total, 64, 1)], axis=0)
     q_two = jnp.where(iota((16, PAD), 1) < OWN, q_two, 0.0)
-    pre_own = inv_a * dot(hot_code, q_two, HIGH)
+    pre_own = inv_a * share_out(hot_code, q_two, 3)
     act, slope_own = gelu_parts(pre_own)
     pads = jnp.zeros((4, PAD), F32)
-    center = dot(hot_code, jnp.concatenate([pads, e_own, pads, pads], axis=0), HIGH)
+    center = share_out(hot_code, jnp.concatenate([pads, e_own, pads, pads], axis=0), 1)
     m_own = jnp.where(iota((PAD, PAD), 0) < CODES, center + act, 0.0)
     m_own = m_own.astype(BF16).astype(F32)
     b_own = tap_rows(taps, m_own)
@@ -380,10 +389,12 @@
     mine = lanes(x, 384)
     w2 = wpad2[:, mine]
     ppart[...] = dot(high, w2) + dot(low, w2)
-    p_copies = [
-        net.start(ppart.at[rows((y + d) % 4, 32)], py.at[d - 1], along_y(d)) for d in range(1, 4)
-    ]
-    q_copies = [net.start(qown, qparts.at[pos], in_plane(a, b)) for a, b in PLANE]
+    p_copies = net.start(
+        [(ppart.at[rows((y + d) % 4, 32)], py.at[d - 1], along_y(d)) for d in range(1, 4)], py
+    )
+    q_copies = net.start(
+        [(qown, qparts.at[pos], in_plane(a, b)) for a, b in PLANE], qparts.at[0:31]
+    )
 
     for j in range(3):
         @pl.when(targets[j] != pos)
@@ -420,11 +431,11 @@
     def column(row):
         return jnp.transpose(row.astype(F32))[:, 0:1].astype(jnp.int32)
 
-    finish(p_copies)
+    p_copies.wait()
     psum[...] = ppart[rows(y, 32)] + py[0] + py[1] + py[2]
-    p_copies = [
-        net.start(psum.at[rows((z + d) % 4, 8)], pz.at[z], along_z(d)) for d in range(1, 8)
-    ]
+    p_copies = net.start(
+        [(psum.at[rows((z + d) % 4, 8)], pz.at[z], along_z(d)) for d in range(1, 8)], pz.at[0:7]
+    )
     pz[z] = psum[rows(z % 4, 8)]
 
     columns = [column(row) for row in index]
@@ -435,7 +446,7 @@
     wide_a[...] = jnp.where(line == column(code_a), 1.0, 0.0).astype(BF16)
     wide_b[...] = jnp.where(line == column(code_b), 1.0, 0.0).astype(BF16)
 
-    finish(q_copies)
+    q_copies.wait()
     for i in range(32):
         tile = qparts[i]
         qfull[0:8, OWN * i : OWN * i + OWN] = tile[:, 0:OWN]
@@ -446,18 +457,21 @@
     sums = jnp.zeros((PAD, 128), F32)
     for b in range(BLOCKS):
         if b == BLOCKS // 2:
-            finish(p_copies)
+            p_copies.wait()
             total = pz[0]
             for i in range(1, 8):
                 total = total + pz[i]
             pmid[z % 4] = total
-            p_copies = [
-                net.start(pmid.at[z % 4], pmid.at[z % 4], along_half_z(d)) for d in range(1, 4)
-            ]
+            p_copies = net.start(
+                [(pmid.at[z % 4], pmid.at[z % 4], along_half_z(d)) for d in range(1, 4)],
+                pmid.at[0:3],
+            )
         here = slice(BLOCK * b, BLOCK * b + BLOCK)
-        pre = inv_a * dot(hot_code, qfull[:, here], HIGH)
+        pre = inv_a * share_out(hot_code, qfull[:, here], 3)
         act, grad = gelu_parts(pre)
-        center = dot(hot_code, jnp.concatenate([pads, emb[:, here], pads, pads], axis=0))
+        center = share_out(
+            hot_code, jnp.concatenate([pads, emb[:, here], pads, pads], axis=0), 1
+        )
         live = iota((PAD, BLOCK), 0) < CODES
         table[:, here] = jnp.where(live, center + act, 0.0).astype(BF16)
         sv = jnp.where(live, grad * (0.5 * dot(mid_t[...], cots[:, here])), 0.0)
@@ -465,18 +479,19 @@
         prod = sv * pre
         sums = sums + prod[:, 0:128] + prod[:, 128:256]
 
-    finish(p_copies)
+    p_copies.wait()
     quarter = pl.ds(pl.multiple_of(c * 128 + y * 32, 32), 32)
     pbuf[quarter, mine] = jnp.concatenate([pmid[i] for i in range(4)], axis=0).astype(BF16)
     block = pbuf.at[quarter, mine]
-    p_copies = [net.start(block, block, in_square(a, b)) for a, b in SQUARE]
-    p_shares = [net.start(block, block, other_core())]
+    p_copies = net.start(
+        [(block, block, in_square(a, b)) for a, b in SQUARE], pbuf.at[0:240, 0:768]
+    )
 
     hot_ct = code_onehot(iota((16, PAD), 1), iota((16, PAD), 0))
-    fv = dot(hot_ct, table_v[...], HIGH)
+    fv = share_out(hot_ct, table_v[...], 2)
     mean_v = jnp.sum(sums, axis=1, keepdims=True) * (1.0 / C)
     hot_gram = code_onehot(iota((PAD, PAD), 0), iota((PAD, PAD), 1) - 96)
-    gram_v = dot(hot_ct, (inv_a * inv_a * mean_v) * hot_gram, HIGH)
+    gram_v = share_out(hot_ct, (inv_a * inv_a * mean_v) * hot_gram, 2)
     xbuf[:, C + ROWS : WIDE] = jnp.zeros((ROWS, WIDE - C - ROWS), F32)
     xbuf[0:16, C + ROWS : C + ROWS + PAD] = gram_v
     for i in range(16):
@@ -506,19 +521,16 @@
         lax.rsqrt(jnp.sum(acc[...], axis=1, keepdims=True) * (1.0 / C) + EPS), (2 * L, 128)
     )
 
-    for copy, (a, b) in zip(p_copies, SQUARE):
-        copy.wait()
-        here = pl.ds(pl.multiple_of(c * 128 + ((y - b + 4) % 4) * 32, 32), 32)
-        block = pbuf.at[here, lanes((x - a + 4) % 4, 384)]
-        p_shares.append(net.start(block, block, other_core()))
-    finish(p_shares)
-
-    base = net.take(BLOCKS)
+    half = rows(c, 128)
+    p_copies.wait()
+    net.start([(pbuf.at[half], pbuf.at[half], other_core())], pbuf.at[half]).wait()
+
+    base = net.take(2)
     away = rows(1 - c, 128)
 
     def core_copy(b):
         here = lanes(b, BLOCK)
-        return net.copy(core_send.at[:, here], from_core.at[:, here], other_core(), base + b)
+        return net.copy(core_send.at[:, here], from_core.at[:, here], other_core(), base + b // 4)
 
     def second_pass(b, carry):
         here = lanes(b, BLOCK)
@@ -545,7 +557,6 @@
         core_copy(b).start()
         return carry
 
-    half = rows(c, 128)
     third = pl.ds(pl.multiple_of(c * 128 + x * 32, 32), 32)
 
     def chip_sum(first, last):
@@ -556,55 +567,52 @@
         return pl.ds(pl.multiple_of(1024 * h + at * 256, 128), 256)
 
     def square_scatter(h):
-        return [
-            net.start(
-                chip_low.at[rows((x + a) % 4, 32), strip(h, (y + b) % 4)], xin.at[h, j], in_square(a, b)
-            )
-            for j, (a, b) in enumerate(SQUARE)
-        ]
+        items = []
+        for j, (a, b) in enumerate(SQUARE):
+            block = chip_low.at[rows((x + a) % 4, 32), strip(h, (y + b) % 4)]
+            items.append((block, xin.at[h, j], in_square(a, b)))
+        return net.start(items, xin.at[h])
 
     def line_scatter(h, copies):
-        finish(copies)
+        copies.wait()
         total = xbuf[third, strip(h, y)]
         for j in range(15):
             total = total + xin[h, j].astype(F32)
         xsum[h, 0] = total[:, 0:128]
         xsum[h, 1] = total[:, 128:256]
-        started = []
+        items = []
         for d in range(1, 8):
             to = (z + d) % 8
             block = xsum.at[h, to // 4, rows(to % 4, 8)]
-            started.append(net.start(block, zin.at[h, d - 1], along_z(d)))
-        return started
+            items.append((block, zin.at[h, d - 1], along_z(d)))
+        return net.start(items, zin.at[h])
 
     def line_gather(h, copies):
-        finish(copies)
+        copies.wait()
         total = xsum[h, z // 4, rows(z % 4, 8)]
         for d in range(7):
             total = total + zin[h, d]
         zout[h, z] = total
-        return [net.start(zout.at[h, z], zout.at[h, z], along_z(d)) for d in range(1, 8)]
+        items = [(zout.at[h, z], zout.at[h, z], along_z(d)) for d in range(1, 8)]
+        return net.start(items, zout.at[h, 0:7])
 
     def square_gather(h, copies):
-        finish(copies)
+        copies.wait()
         for i in range(2):
             here = pl.ds(pl.multiple_of(1024 * h + y * 256 + 128 * i, 128), 128)
             tiles = [zout[h, 4 * i + q] for q in range(4)]
             full[third, here] = jnp.concatenate(tiles, axis=0).astype(BF16)
         block = full.at[third, strip(h, y)]
-        shares = [net.start(block, block, other_core())]
-        return [net.start(block, block, in_square(a, b)) for a, b in SQUARE], shares
-
-    def share(h, copies, shares):
-        for copy, (a, b) in zip(copies, SQUARE):
-            copy.wait()
-            here = pl.ds(pl.multiple_of(c * 128 + ((x - a + 4) % 4) * 32, 32), 32)
-            block = full.at[here, strip(h, (y - b + 4) % 4)]
-            shares.append(net.start(block, block, other_core()))
+        items = [(block, block, in_square(a, b)) for a, b in SQUARE]
+        return net.start(items, full.at[0:240, 0:512])
+
+    def share(h, copies):
+        copies.wait()
+        block = full.at[half, 1024 * h : 1024 * h + 1024]
+        return net.start([(block, block, other_core())], block)
 
     lax.fori_loop(0, 4, second_pass, 0)
-    for b in range(4):
-        core_copy(b).wait()
+    net.copy(core_send.at[:, 0:1024], from_core.at[:, 0:1024], other_core(), base).wait()
     chip_sum(0, 1024)
     scatter_0 = square_scatter(0)
     lax.fori_loop(4, BLOCKS, second_pass, 0)
@@ -614,14 +622,14 @@
     high, low = split(weight * hot[...].astype(F32))
     xbuf[:, C : C + ROWS] = dot(hot_t[...], high) + dot(hot_t[...], low)
     core_send[:, C:WIDE] = xbuf[away, C:WIDE].astype(BF16)
-    last = net.start(core_send.at[:, C:WIDE], from_core.at[:, C:WIDE], other_core())
-    for b in range(4, BLOCKS):
-        core_copy(b).wait()
-    chip_sum(1024, C)
-    last.wait()
-    chip_sum(C, WIDE)
+    net.copy(core_send.at[:, C:WIDE], from_core.at[:, C:WIDE], other_core(), base + 1).start()
+    net.copy(core_send.at[:, 1024:WIDE], from_core.at[:, 1024:WIDE], other_core(), base + 1).wait()
+    chip_sum(1024, WIDE)
     scatter_1 = square_scatter(1)
     line_0 = line_scatter(0, scatter_0)
+
+    gather_0 = line_gather(0, line_0)
+    line_1 = line_scatter(1, scatter_1)
 
     def third_pass(b, carry):
         here = lanes(b, BLOCK)
@@ -634,13 +642,10 @@
     store = pltpu.make_async_copy(out_buf, out_out, lsem.at[9])
     store.start()
 
-    gather_0 = line_gather(0, line_0)
-    line_1 = line_scatter(1, scatter_1)
-    back_0, shares_0 = square_gather(0, gather_0)
+    back_0 = square_gather(0, gather_0)
     gather_1 = line_gather(1, line_1)
-    back_1, shares_1 = square_gather(1, gather_1)
-    share(0, back_0, shares_0)
-    finish(shares_0)
+    back_1 = square_gather(1, gather_1)
+    shares = share(0, back_0)
     turned_high, turned_low = split(jnp.transpose(a_own))
     both = jnp.concatenate([turned_high[0:OWN], turned_low[0:OWN]], axis=0)
 
@@ -648,12 +653,13 @@
         grad = dot(both, full[:, b : b + 512])
         gw_ref[OWN : 2 * OWN, b : b + 512] = grad[0:OWN] + grad[OWN : 2 * OWN]
 
+    shares.wait()
     ew = dot_nt(full[:, 0:1024], wpad2[:, 0:1024])
+    shares = share(1, back_1)
     grad_b(0)
     grad_b(512)
     fbuf[...] = jnp.zeros_like(fbuf)
-    share(1, back_1, shares_1)
-    finish(shares_1)
+    shares.wait()
 
     ew = ew + dot_nt(full[:, 1024:C], wpad2[:, 1024:C])
     high, low = split(b_own)
@@ -682,16 +688,16 @@
     fv = full[pl.ds(pl.multiple_of((pos // 2) * 16, 16), 16), extra : extra + PAD].astype(F32)
     fv = jnp.where(pos % 2 == 1, pltpu.roll(fv, PAD - OWN, 1), fv)
     fv = jnp.where(iota((16, PAD), 1) < OWN, fv, 0.0)
-    own_rows = fv + dot(narrow, inv * s, HIGH)
+    own_rows = fv + share_out(narrow, inv * s, 2)
     f_rows = jnp.where(iota((16, PAD), 0) < 12, own_rows, 0.0)
     vec_rows = jnp.concatenate([jnp.zeros((12, PAD), F32)] + taps_b + [gain_b], axis=0)
-    packet = f_rows + vec_rows + dot(narrow, (inv * inv * mean_s) * hot_far, HIGH)
+    packet = f_rows + vec_rows + share_out(narrow, (inv * inv * mean_s) * hot_far, 2)
     pack[...] = packet[0:8] + pltpu.roll(packet[8:16], 64, 1)
     packs[pos] = pack[...]
-    copies = [net.start(pack, packs.at[pos], in_plane(a, b)) for a, b in PLANE]
+    copies = net.start([(pack, packs.at[pos], in_plane(a, b)) for a, b in PLANE], packs.at[0:31])
 
     grad_b(1024)
-    finish(copies)
+    copies.wait()
     total = jnp.zeros((8, PAD), F32)
     for i in range(32):
         tile = packs[i]
@@ -718,14 +724,19 @@
         axis=0,
     )
     packs2[pos] = pack2[...]
-    copies = [net.start(pack2, packs2.at[pos], in_plane(a, b)) for a, b in PLANE]
+    copies = net.start(
+        [(pack2, packs2.at[pos], in_plane(a, b)) for a, b in PLANE], packs2.at[0:31]
+    )
 
     wide = jnp.concatenate([g1_own * te_own, jnp.zeros((PAD - 16, PAD), F32)], axis=0)
-    wide = jnp.transpose(wide)
+    wide_high, wide_low = split(jnp.transpose(wide)[0:OWN])
+    wide = jnp.concatenate([wide_high, wide_low], axis=0)
     for b in range(0, C, 512):
-        gw_ref[0:OWN, b : b + 512] = dot(wide, fbuf[:, b : b + 512], HIGH)[0:OWN]
+        f_high, f_low = split(fbuf[:, b : b + 512])
+        grad = dot(wide, f_high)
+        gw_ref[0:OWN, b : b + 512] = grad[0:OWN] + grad[OWN : 2 * OWN] + dot(wide_high, f_low)
     vec_ref[4:8, :] = fbuf[12:16, :]
-    finish(copies)
+    copies.wait()
     for i in range(32):
         tile = packs2[i]
         here = slice(OWN * i, OWN * i + OWN)
@@ -805,8 +816,8 @@
             pltpu.VMEM((32, 2, PAD), F32),
             pltpu.SemaphoreType.DMA((10,)),
             pltpu.SemaphoreType.DMA((2, 3)),
-            pltpu.SemaphoreType.DMA((320,)),
-            pltpu.SemaphoreType.DMA((320,)),
+            pltpu.SemaphoreType.DMA((24,)),
+            pltpu.SemaphoreType.DMA((24,)),
         ],
         compiler_params=pltpu.CompilerParams(
             collective_id=0, has_side_effects=True, vmem_limit_bytes=62 * 2**20

time: 99 us -> 94 us (0.949)
  Pallas kernels: 98.2 us -> 93.2 us
    pallas_call x1, Pallas kernels: 95.7 us -> 90.7 us  [whole(): pl.pallas_call(whole_kernel, out_shape=(jax.ShapeDtypeStruct((L, C), BF16...]
where the time goes in v4:
time: 94 us; the launch traced here: 93.8 us
  Pallas kernels  93.2 us (99%)
    pallas_call x1, Pallas kernels, whole(): pl.pallas_call(whole_kernel, out_shape=(jax.ShapeDtypeStruct((L, C), BF16...  90.7 us
    pallas_call x1, Pallas kernels, placed_outputs(): pl.pallas_call(place_kernel, out_shape=(jax.ShapeDtypeStruct((L, C), BF16...  2.43 us

profile of v4, /device:TPU:1, one launch (start us, length us, event | category | flops | bytes accessed | tf_op | source)
XLA Modules:
  0.0 93.8 jit_solution(12390911212945648936)
XLA Ops:
  0.6 90.7 %whole.1 = (bf16[256,1536]{1,0:T(8,128)(2,1)}, f32[96,1536]{1,0:T(8,128)}, f32[8,1536]{1,0:T(8,128)}) custom-call(s32[1,256]{1,0:T(1,128)} %tok_in.1, bf16[4,1536]{1,0:T(4,128)(2,1)} %emb_in.1, f32[3,1536]{1,0:T(4,128)} %k1_in.1, f32[1536]{0:T(1024)} %g1_in.1, bf16[48,1536]{1,0:T(8,128)(2,1)} %w1_in.1, f32[3,1536]{1,0:T(4,128)} %k2_in.1, f32[1536]{0:T(1024)} %g2_in.1, ...), custom_call_target="tpu_custom_call" | custom-call | tf_op jit(solution)/shard_map/whole/pallas_call | solution.py:754
  91.4 2.4 %place.1 = (bf16[256,1536]{1,0:T(8,128)(2,1)}, f32[48,1536]{1,0:T(8,128)}, f32[48,1536]{1,0:T(8,128)}, f32[3,1536]{1,0:T(4,128)}, f32[3,1536]{1,0:T(4,128)}, /*index=5*/f32[1536]{0:T(1024)}, f32[1536]{0:T(1024)}) custom-call(bf16[256,1536]{1,0:T(8,128)(2,1)} %get-tuple-element.17.out_in, f32[96,1536]{1,0:T(8,128)} %get-tuple-element.18.gw_in, ...), custom_call_target="tpu_custom_call" | custom-call | tf_op jit(solution)/shard_map/place/pallas_call | solution.py:841

commit v5 on v4

--- a/solution.py
+++ b/solution.py
@@ -31,45 +31,17 @@
     pos = lax.axis_index("pos")
     strand = lax.axis_index("strand")
     rep = lax.axis_index("rep")
-    return pos // 8, pos % 8, (rep // 2) * 2 + strand, rep % 2
-
-
-def device(y, z, x, c):
-    return {"pos": y * 8 + z, "strand": x % 2, "rep": (x // 2) * 2 + c}
-
-
-def along_y(d):
-    y, z, x, c = coords()
-    return device((y + d) % 4, z, x, c)
-
-
-def along_z(d):
-    y, z, x, c = coords()
-    return device(y, (z + d) % 8, x, c)
-
-
-def along_half_z(d):
-    y, z, x, c = coords()
-    return device(y, (z // 4) * 4 + (z + d) % 4, x, c)
-
-
-def other_core():
-    y, z, x, c = coords()
-    return device(y, z, x, 1 - c)
+    high, core = lax.div(rep, 2), lax.rem(rep, 2)
+    return lax.div(pos, 8), lax.rem(pos, 8), high * 2 + strand, core
 
 
 PLANE = [(a, b) for a in range(4) for b in range(8) if a or b]
 SQUARE = [(a, b) for a in range(4) for b in range(4) if a or b]
 
 
-def in_plane(a, b):
-    y, z, x, c = coords()
-    return device((y + a) % 4, (z + b) % 8, x, c)
-
-
-def in_square(a, b):
-    y, z, x, c = coords()
-    return device((y + b) % 4, z, (x + a) % 4, c)
+def wrapped(at, size):
+    moved = [at] + [at + d for d in range(1, size)]
+    return [at] + [jnp.where(m >= size, m - size, m) for m in moved[1:]]
 
 
 class Net:
@@ -95,7 +67,7 @@
         sem = self.take(1)
         for src, dst, to in items:
             self.copy(src, dst, to, sem).start()
-        return self.copy(total, total, other_core(), sem)
+        return self.copy(total, total, items[0][2], sem)
 
 
 def share_out(onehot, value, parts):
@@ -238,9 +210,7 @@
     from_core,
     chip_low,
     xin,
-    xsum,
     zin,
-    zout,
     full,
     pack,
     packs,
@@ -256,6 +226,21 @@
     pos = lax.axis_index("pos")
     strand = lax.axis_index("strand")
     rep = lax.axis_index("rep")
+    ys, zs, xs = wrapped(y, 4), wrapped(z, 8), wrapped(x, 4)
+    zq = lax.rem(z, 4)
+    zqs = wrapped(zq, 4)
+    xsr = [(lax.rem(v, 2), lax.div(v, 2) * 2 + c) for v in xs]
+    xsr[0] = (strand, rep)
+
+    def peer_at(a, b, e):
+        return {"pos": ys[a] * 8 + zs[b], "strand": xsr[e][0], "rep": xsr[e][1]}
+
+    plane_ids = [peer_at(a, b, 0) for a, b in PLANE]
+    square_ids = [peer_at(b, 0, a) for a, b in SQUARE]
+    y_ids = [peer_at(d, 0, 0) for d in range(4)]
+    z_ids = [peer_at(0, d, 0) for d in range(8)]
+    hz_ids = [{"pos": pos - zq + zqs[d], "strand": strand, "rep": rep} for d in range(4)]
+    core_id = {"pos": pos, "strand": strand, "rep": rep + 1 - 2 * c}
     frame = jnp.where(strand == 1, 31 - pos, pos)
     targets = [(frame + d + 32) % 32 for d in (-1, 0, 1)]
     net = Net(send, recv)
@@ -282,11 +267,7 @@
         load.start()
 
     barrier = pltpu.get_barrier_semaphore()
-    peers = (
-        [in_plane(a, b) for a, b in PLANE]
-        + [in_square(a, b) for a, b in SQUARE if a]
-        + [other_core()]
-    )
+    peers = plane_ids + [i for i, (a, b) in zip(square_ids, SQUARE) if a] + [core_id]
     for peer in peers:
         pl.semaphore_signal(barrier, inc=1, device_id=peer, device_id_type=MESH)
 
@@ -316,8 +297,8 @@
 
     q_copies = net.start(
         [
-            (qsend.at[((y + a) % 4) * 8 + (z + b) % 8], qrecv.at[pos], in_plane(a, b))
-            for a, b in PLANE
+            (qsend.at[to["pos"]], qrecv.at[pos], to)
+            for to in plane_ids
         ],
         qrecv.at[0:31],
     )
@@ -390,10 +371,10 @@
     w2 = wpad2[:, mine]
     ppart[...] = dot(high, w2) + dot(low, w2)
     p_copies = net.start(
-        [(ppart.at[rows((y + d) % 4, 32)], py.at[d - 1], along_y(d)) for d in range(1, 4)], py
+        [(ppart.at[rows(ys[d], 32)], py.at[d - 1], y_ids[d]) for d in range(1, 4)], py
     )
     q_copies = net.start(
-        [(qown, qparts.at[pos], in_plane(a, b)) for a, b in PLANE], qparts.at[0:31]
+        [(qown, qparts.at[pos], to) for to in plane_ids], qparts.at[0:31]
     )
 
     for j in range(3):
@@ -434,9 +415,9 @@
     p_copies.wait()
     psum[...] = ppart[rows(y, 32)] + py[0] + py[1] + py[2]
     p_copies = net.start(
-        [(psum.at[rows((z + d) % 4, 8)], pz.at[z], along_z(d)) for d in range(1, 8)], pz.at[0:7]
-    )
-    pz[z] = psum[rows(z % 4, 8)]
+        [(psum.at[rows(zqs[d % 4], 8)], pz.at[z], z_ids[d]) for d in range(1, 8)], pz.at[0:7]
+    )
+    pz[z] = psum[rows(zq, 8)]
 
     columns = [column(row) for row in index]
     line = iota((2 * L, ROWS), 1)
@@ -461,9 +442,9 @@
             total = pz[0]
             for i in range(1, 8):
                 total = total + pz[i]
-            pmid[z % 4] = total
+            pmid[zq] = total
             p_copies = net.start(
-                [(pmid.at[z % 4], pmid.at[z % 4], along_half_z(d)) for d in range(1, 4)],
+                [(pmid.at[zq], pmid.at[zq], hz_ids[d]) for d in range(1, 4)],
                 pmid.at[0:3],
             )
         here = slice(BLOCK * b, BLOCK * b + BLOCK)
@@ -484,7 +465,7 @@
     pbuf[quarter, mine] = jnp.concatenate([pmid[i] for i in range(4)], axis=0).astype(BF16)
     block = pbuf.at[quarter, mine]
     p_copies = net.start(
-        [(block, block, in_square(a, b)) for a, b in SQUARE], pbuf.at[0:240, 0:768]
+        [(block, block, to) for to in square_ids], pbuf.at[0:240, 0:768]
     )
 
     hot_ct = code_onehot(iota((16, PAD), 1), iota((16, PAD), 0))
@@ -523,14 +504,14 @@
 
     half = rows(c, 128)
     p_copies.wait()
-    net.start([(pbuf.at[half], pbuf.at[half], other_core())], pbuf.at[half]).wait()
+    net.start([(pbuf.at[half], pbuf.at[half], core_id)], pbuf.at[half]).wait()
 
     base = net.take(2)
     away = rows(1 - c, 128)
 
     def core_copy(b):
         here = lanes(b, BLOCK)
-        return net.copy(core_send.at[:, here], from_core.at[:, here], other_core(), base + b // 4)
+        return net.copy(core_send.at[:, here], from_core.at[:, here], core_id, base + b // 4)
 
     def second_pass(b, carry):
         here = lanes(b, BLOCK)
@@ -569,67 +550,49 @@
     def square_scatter(h):
         items = []
         for j, (a, b) in enumerate(SQUARE):
-            block = chip_low.at[rows((x + a) % 4, 32), strip(h, (y + b) % 4)]
-            items.append((block, xin.at[h, j], in_square(a, b)))
+            block = chip_low.at[rows(xs[a], 32), strip(h, ys[b])]
+            items.append((block, xin.at[h, j], square_ids[j]))
         return net.start(items, xin.at[h])
 
-    def line_scatter(h, copies):
+    def line_all(h, copies):
         copies.wait()
         total = xbuf[third, strip(h, y)]
         for j in range(15):
             total = total + xin[h, j].astype(F32)
-        xsum[h, 0] = total[:, 0:128]
-        xsum[h, 1] = total[:, 128:256]
-        items = []
-        for d in range(1, 8):
-            to = (z + d) % 8
-            block = xsum.at[h, to // 4, rows(to % 4, 8)]
-            items.append((block, zin.at[h, d - 1], along_z(d)))
-        return net.start(items, zin.at[h])
-
-    def line_gather(h, copies):
-        copies.wait()
-        total = xsum[h, z // 4, rows(z % 4, 8)]
-        for d in range(7):
-            total = total + zin[h, d]
-        zout[h, z] = total
-        items = [(zout.at[h, z], zout.at[h, z], along_z(d)) for d in range(1, 8)]
-        return net.start(items, zout.at[h, 0:7])
+        zin[h, z] = total.astype(BF16)
+        block = zin.at[h, z]
+        return net.start([(block, block, to) for to in z_ids[1:]], zin.at[h, 0:7])
 
     def square_gather(h, copies):
         copies.wait()
-        for i in range(2):
-            here = pl.ds(pl.multiple_of(1024 * h + y * 256 + 128 * i, 128), 128)
-            tiles = [zout[h, 4 * i + q] for q in range(4)]
-            full[third, here] = jnp.concatenate(tiles, axis=0).astype(BF16)
+        total = zin[h, 0].astype(F32)
+        for d in range(1, 8):
+            total = total + zin[h, d].astype(F32)
+        full[third, strip(h, y)] = total.astype(BF16)
         block = full.at[third, strip(h, y)]
-        items = [(block, block, in_square(a, b)) for a, b in SQUARE]
+        items = [(block, block, to) for to in square_ids]
         return net.start(items, full.at[0:240, 0:512])
 
     def share(h, copies):
         copies.wait()
         block = full.at[half, 1024 * h : 1024 * h + 1024]
-        return net.start([(block, block, other_core())], block)
+        return net.start([(block, block, core_id)], block)
 
     lax.fori_loop(0, 4, second_pass, 0)
-    net.copy(core_send.at[:, 0:1024], from_core.at[:, 0:1024], other_core(), base).wait()
+    net.copy(core_send.at[:, 0:1024], from_core.at[:, 0:1024], core_id, base).wait()
     chip_sum(0, 1024)
     scatter_0 = square_scatter(0)
     lax.fori_loop(4, BLOCKS, second_pass, 0)
 
     inv = acc[:, 0:1]
     weight = (0.5 / C) * inv * inv * jnp.sum(acc2[...], axis=1, keepdims=True)
-    high, low = split(weight * hot[...].astype(F32))
-    xbuf[:, C : C + ROWS] = dot(hot_t[...], high) + dot(hot_t[...], low)
+    xbuf[:, C : C + ROWS] = dot(hot_t[...], (weight * hot[...].astype(F32)).astype(BF16))
     core_send[:, C:WIDE] = xbuf[away, C:WIDE].astype(BF16)
-    net.copy(core_send.at[:, C:WIDE], from_core.at[:, C:WIDE], other_core(), base + 1).start()
-    net.copy(core_send.at[:, 1024:WIDE], from_core.at[:, 1024:WIDE], other_core(), base + 1).wait()
+    net.copy(core_send.at[:, C:WIDE], from_core.at[:, C:WIDE], core_id, base + 1).start()
+    net.copy(core_send.at[:, 1024:WIDE], from_core.at[:, 1024:WIDE], core_id, base + 1).wait()
     chip_sum(1024, WIDE)
     scatter_1 = square_scatter(1)
-    line_0 = line_scatter(0, scatter_0)
-
-    gather_0 = line_gather(0, line_0)
-    line_1 = line_scatter(1, scatter_1)
+    line_0 = line_all(0, scatter_0)
 
     def third_pass(b, carry):
         here = lanes(b, BLOCK)
@@ -642,9 +605,9 @@
     store = pltpu.make_async_copy(out_buf, out_out, lsem.at[9])
     store.start()
 
-    back_0 = square_gather(0, gather_0)
-    gather_1 = line_gather(1, line_1)
-    back_1 = square_gather(1, gather_1)
+    line_1 = line_all(1, scatter_1)
+    back_0 = square_gather(0, line_0)
+    back_1 = square_gather(1, line_1)
     shares = share(0, back_0)
     turned_high, turned_low = split(jnp.transpose(a_own))
     both = jnp.concatenate([turned_high[0:OWN], turned_low[0:OWN]], axis=0)
@@ -694,7 +657,7 @@
     packet = f_rows + vec_rows + share_out(narrow, (inv * inv * mean_s) * hot_far, 2)
     pack[...] = packet[0:8] + pltpu.roll(packet[8:16], 64, 1)
     packs[pos] = pack[...]
-    copies = net.start([(pack, packs.at[pos], in_plane(a, b)) for a, b in PLANE], packs.at[0:31])
+    copies = net.start([(pack, packs.at[pos], to) for to in plane_ids], packs.at[0:31])
 
     grad_b(1024)
     copies.wait()
@@ -725,7 +688,7 @@
     )
     packs2[pos] = pack2[...]
     copies = net.start(
-        [(pack2, packs2.at[pos], in_plane(a, b)) for a, b in PLANE], packs2.at[0:31]
+        [(pack2, packs2.at[pos], to) for to in plane_ids], packs2.at[0:31]
     )
 
     wide = jnp.concatenate([g1_own * te_own, jnp.zeros((PAD - 16, PAD), F32)], axis=0)
@@ -805,9 +768,7 @@
             pltpu.VMEM((128, WIDE), BF16),
             pltpu.VMEM((128, WIDE), BF16),
             pltpu.VMEM((2, 15, 32, 256), BF16),
-            pltpu.VMEM((2, 2, 32, 128), F32),
-            pltpu.VMEM((2, 7, 8, 128), F32),
-            pltpu.VMEM((2, 8, 8, 128), F32),
+            pltpu.VMEM((2, 8, 32, 256), BF16),
             pltpu.VMEM((ROWS, WIDE), BF16),
             pltpu.VMEM((8, PAD), F32),
             pltpu.VMEM((32, 8, PAD), F32),

time: 94 us -> 89.1 us (0.948)
  Pallas kernels: 93.2 us -> 88.3 us
    pallas_call x1, Pallas kernels: 90.7 us -> 85.8 us  [whole(): pl.pallas_call(whole_kernel, out_shape=(jax.ShapeDtypeStruct((L, C), BF16...]
where the time goes in v5:
time: 89.1 us; the launch traced here: 88.9 us
  Pallas kernels  88.3 us (99%)
    pallas_call x1, Pallas kernels, whole(): pl.pallas_call(whole_kernel, out_shape=(jax.ShapeDtypeStruct((L, C), BF16...  85.8 us
    pallas_call x1, Pallas kernels, placed_outputs(): pl.pallas_call(place_kernel, out_shape=(jax.ShapeDtypeStruct((L, C), BF16...  2.43 us

profile of v5, /device:TPU:1, one launch (start us, length us, event | category | flops | bytes accessed | tf_op | source)
XLA Modules:
  0.0 88.9 jit_solution(9753589191127501107)
XLA Ops:
  0.6 85.8 %whole.1 = (bf16[256,1536]{1,0:T(8,128)(2,1)}, f32[96,1536]{1,0:T(8,128)}, f32[8,1536]{1,0:T(8,128)}) custom-call(s32[1,256]{1,0:T(1,128)} %tok_in.1, bf16[4,1536]{1,0:T(4,128)(2,1)} %emb_in.1, f32[3,1536]{1,0:T(4,128)} %k1_in.1, f32[1536]{0:T(1024)} %g1_in.1, bf16[48,1536]{1,0:T(8,128)(2,1)} %w1_in.1, f32[3,1536]{1,0:T(4,128)} %k2_in.1, f32[1536]{0:T(1024)} %g2_in.1, ...), custom_call_target="tpu_custom_call" | custom-call | tf_op jit(solution)/shard_map/whole/pallas_call | solution.py:717
  86.5 2.4 %place.1 = (bf16[256,1536]{1,0:T(8,128)(2,1)}, f32[48,1536]{1,0:T(8,128)}, f32[48,1536]{1,0:T(8,128)}, f32[3,1536]{1,0:T(4,128)}, f32[3,1536]{1,0:T(4,128)}, /*index=5*/f32[1536]{0:T(1024)}, f32[1536]{0:T(1024)}) custom-call(bf16[256,1536]{1,0:T(8,128)(2,1)} %get-tuple-element.17.out_in, f32[96,1536]{1,0:T(8,128)} %get-tuple-element.18.gw_in, ...), custom_call_target="tpu_custom_call" | custom-call | tf_op jit(solution)/shard_map/place/pallas_call | solution.py:802

commit v6 on v5

--- a/solution.py
+++ b/solution.py
@@ -185,9 +185,7 @@
     aown,
     ppart,
     py,
-    psum,
     pz,
-    pmid,
     pbuf,
     table,
     table_slope,
@@ -227,8 +225,6 @@
     strand = lax.axis_index("strand")
     rep = lax.axis_index("rep")
     ys, zs, xs = wrapped(y, 4), wrapped(z, 8), wrapped(x, 4)
-    zq = lax.rem(z, 4)
-    zqs = wrapped(zq, 4)
     xsr = [(lax.rem(v, 2), lax.div(v, 2) * 2 + c) for v in xs]
     xsr[0] = (strand, rep)
 
@@ -239,7 +235,6 @@
     square_ids = [peer_at(b, 0, a) for a, b in SQUARE]
     y_ids = [peer_at(d, 0, 0) for d in range(4)]
     z_ids = [peer_at(0, d, 0) for d in range(8)]
-    hz_ids = [{"pos": pos - zq + zqs[d], "strand": strand, "rep": rep} for d in range(4)]
     core_id = {"pos": pos, "strand": strand, "rep": rep + 1 - 2 * c}
     frame = jnp.where(strand == 1, 31 - pos, pos)
     targets = [(frame + d + 32) % 32 for d in (-1, 0, 1)]
@@ -413,11 +408,8 @@
         return jnp.transpose(row.astype(F32))[:, 0:1].astype(jnp.int32)
 
     p_copies.wait()
-    psum[...] = ppart[rows(y, 32)] + py[0] + py[1] + py[2]
-    p_copies = net.start(
-        [(psum.at[rows(zqs[d % 4], 8)], pz.at[z], z_ids[d]) for d in range(1, 8)], pz.at[0:7]
-    )
-    pz[z] = psum[rows(zq, 8)]
+    pz[z] = (ppart[rows(y, 32)] + py[0] + py[1] + py[2]).astype(BF16)
+    p_copies = net.start([(pz.at[z], pz.at[z], to) for to in z_ids[1:]], pz.at[0:7])
 
     columns = [column(row) for row in index]
     line = iota((2 * L, ROWS), 1)
@@ -437,16 +429,6 @@
     pads = jnp.zeros((4, BLOCK), F32)
     sums = jnp.zeros((PAD, 128), F32)
     for b in range(BLOCKS):
-        if b == BLOCKS // 2:
-            p_copies.wait()
-            total = pz[0]
-            for i in range(1, 8):
-                total = total + pz[i]
-            pmid[zq] = total
-            p_copies = net.start(
-                [(pmid.at[zq], pmid.at[zq], hz_ids[d]) for d in range(1, 4)],
-                pmid.at[0:3],
-            )
         here = slice(BLOCK * b, BLOCK * b + BLOCK)
         pre = inv_a * share_out(hot_code, qfull[:, here], 3)
         act, grad = gelu_parts(pre)
@@ -462,7 +444,10 @@
 
     p_copies.wait()
     quarter = pl.ds(pl.multiple_of(c * 128 + y * 32, 32), 32)
-    pbuf[quarter, mine] = jnp.concatenate([pmid[i] for i in range(4)], axis=0).astype(BF16)
+    total = pz[0].astype(F32)
+    for i in range(1, 8):
+        total = total + pz[i].astype(F32)
+    pbuf[quarter, mine] = total.astype(BF16)
     block = pbuf.at[quarter, mine]
     p_copies = net.start(
         [(block, block, to) for to in square_ids], pbuf.at[0:240, 0:768]
@@ -578,11 +563,11 @@
         block = full.at[half, 1024 * h : 1024 * h + 1024]
         return net.start([(block, block, core_id)], block)
 
-    lax.fori_loop(0, 4, second_pass, 0)
+    lax.fori_loop(0, 5, second_pass, 0)
     net.copy(core_send.at[:, 0:1024], from_core.at[:, 0:1024], core_id, base).wait()
     chip_sum(0, 1024)
     scatter_0 = square_scatter(0)
-    lax.fori_loop(4, BLOCKS, second_pass, 0)
+    lax.fori_loop(5, BLOCKS, second_pass, 0)
 
     inv = acc[:, 0:1]
     weight = (0.5 / C) * inv * inv * jnp.sum(acc2[...], axis=1, keepdims=True)
@@ -743,9 +728,7 @@
             pltpu.VMEM((ROWS, PAD), F32),
             pltpu.VMEM((128, 384), F32),
             pltpu.VMEM((3, 32, 384), F32),
-            pltpu.VMEM((32, 384), F32),
-            pltpu.VMEM((8, 8, 384), F32),
-            pltpu.VMEM((4, 8, 384), F32),
+            pltpu.VMEM((8, 32, 384), BF16),
             pltpu.VMEM((ROWS, C), BF16),
             pltpu.VMEM((PAD, C), BF16),
             pltpu.VMEM((8, PAD), F32),

time: 89.1 us -> 84.7 us (0.951)
  Pallas kernels: 88.3 us -> 83.9 us
    pallas_call x1, Pallas kernels: 85.8 us -> 81.4 us  [whole(): pl.pallas_call(whole_kernel, out_shape=(jax.ShapeDtypeStruct((L, C), BF16...]
where the time goes in v6:
time: 84.7 us; the launch traced here: 84.5 us
  Pallas kernels  83.9 us (99%)
    pallas_call x1, Pallas kernels, whole(): pl.pallas_call(whole_kernel, out_shape=(jax.ShapeDtypeStruct((L, C), BF16...  81.4 us
    pallas_call x1, Pallas kernels, placed_outputs(): pl.pallas_call(place_kernel, out_shape=(jax.ShapeDtypeStruct((L, C), BF16...  2.43 us

profile of v6, /device:TPU:1, one launch (start us, length us, event | category | flops | bytes accessed | tf_op | source)
XLA Modules:
  0.0 84.5 jit_solution(10851286335930641344)
XLA Ops:
  0.6 81.4 %whole.1 = (bf16[256,1536]{1,0:T(8,128)(2,1)}, f32[96,1536]{1,0:T(8,128)}, f32[8,1536]{1,0:T(8,128)}) custom-call(s32[1,256]{1,0:T(1,128)} %tok_in.1, bf16[4,1536]{1,0:T(4,128)(2,1)} %emb_in.1, f32[3,1536]{1,0:T(4,128)} %k1_in.1, f32[1536]{0:T(1024)} %g1_in.1, bf16[48,1536]{1,0:T(8,128)(2,1)} %w1_in.1, f32[3,1536]{1,0:T(4,128)} %k2_in.1, f32[1536]{0:T(1024)} %g2_in.1, ...), custom_call_target="tpu_custom_call" | custom-call | tf_op jit(solution)/shard_map/whole/pallas_call | solution.py:702
  82.1 2.4 %place.1 = (bf16[256,1536]{1,0:T(8,128)(2,1)}, f32[48,1536]{1,0:T(8,128)}, f32[48,1536]{1,0:T(8,128)}, f32[3,1536]{1,0:T(4,128)}, f32[3,1536]{1,0:T(4,128)}, /*index=5*/f32[1536]{0:T(1024)}, f32[1536]{0:T(1024)}) custom-call(bf16[256,1536]{1,0:T(8,128)(2,1)} %get-tuple-element.17.out_in, f32[96,1536]{1,0:T(8,128)} %get-tuple-element.18.gw_in, ...), custom_call_target="tpu_custom_call" | custom-call | tf_op jit(solution)/shard_map/place/pallas_call | solution.py:785

commit v7 on v6

--- a/solution.py
+++ b/solution.py
@@ -184,6 +184,7 @@
     qfull,
     aown,
     ppart,
+    plow,
     py,
     pz,
     pbuf,
@@ -365,8 +366,9 @@
     mine = lanes(x, 384)
     w2 = wpad2[:, mine]
     ppart[...] = dot(high, w2) + dot(low, w2)
+    plow[...] = ppart[...].astype(BF16)
     p_copies = net.start(
-        [(ppart.at[rows(ys[d], 32)], py.at[d - 1], y_ids[d]) for d in range(1, 4)], py
+        [(plow.at[rows(ys[d], 32)], py.at[d - 1], y_ids[d]) for d in range(1, 4)], py
     )
     q_copies = net.start(
         [(qown, qparts.at[pos], to) for to in plane_ids], qparts.at[0:31]
@@ -408,7 +410,10 @@
         return jnp.transpose(row.astype(F32))[:, 0:1].astype(jnp.int32)
 
     p_copies.wait()
-    pz[z] = (ppart[rows(y, 32)] + py[0] + py[1] + py[2]).astype(BF16)
+    total = ppart[rows(y, 32)]
+    for i in range(3):
+        total = total + py[i].astype(F32)
+    pz[z] = total.astype(BF16)
     p_copies = net.start([(pz.at[z], pz.at[z], to) for to in z_ids[1:]], pz.at[0:7])
 
     columns = [column(row) for row in index]
@@ -517,7 +522,7 @@
             acc2[some] = kept
             return carry
 
-        lax.fori_loop(0, 8, chunk, 0)
+        lax.fori_loop(0, 8, chunk, 0, unroll=4)
         xbuf[:, here] = 0.5 * dot(hot_t[...], slope[...])
         core_send[:, here] = xbuf[away, here].astype(BF16)
         core_copy(b).start()
@@ -612,7 +617,8 @@
     ew = ew + dot_nt(full[:, 1024:C], wpad2[:, 1024:C])
     high, low = split(b_own)
     gram = full[:, C : C + ROWS]
-    d = g2_own * ew - (dot(gram, high) + dot(gram, low))
+    fix = dot(gram, jnp.concatenate([high, low], axis=1))
+    d = g2_own * ew - (fix[:, 0:PAD] + fix[:, PAD : 2 * PAD])
 
     def total_rows(value):
         return jnp.sum(value, axis=0, keepdims=True)
@@ -661,7 +667,10 @@
     spread = jnp.concatenate(
         [jnp.zeros((OWN, PAD), F32), te_own, jnp.zeros((64, PAD), F32)], axis=0
     )
-    da = g1_own * fw - dot(far, spread, HIGH)
+    far_high, far_low = split(far)
+    spread_high, spread_low = split(spread)
+    fix = dot(jnp.concatenate([far_high, far_low], axis=0), spread_high)
+    da = g1_own * fw - (fix[0:16] + fix[16:32] + dot(far_high, spread_low))
     rows_a = [total_rows(e_own * da[4 * k : 4 * k + 4]) for k in range(3)]
     rows_a = rows_a + [total_rows(te_own * fw)]
     pack2[...] = jnp.concatenate(
@@ -727,7 +736,8 @@
             pltpu.VMEM((16, C), F32),
             pltpu.VMEM((ROWS, PAD), F32),
             pltpu.VMEM((128, 384), F32),
-            pltpu.VMEM((3, 32, 384), F32),
+            pltpu.VMEM((128, 384), BF16),
+            pltpu.VMEM((3, 32, 384), BF16),
             pltpu.VMEM((8, 32, 384), BF16),
             pltpu.VMEM((ROWS, C), BF16),
             pltpu.VMEM((PAD, C), BF16),

time: 84.7 us -> 84.6 us (level)
  no operation moved by 1% of the time
where the time goes in v7:
time: 84.6 us; the launch traced here: 84.4 us
  Pallas kernels  83.8 us (99%)
    pallas_call x1, Pallas kernels, whole(): pl.pallas_call(whole_kernel, out_shape=(jax.ShapeDtypeStruct((L, C), BF16...  81.4 us
    pallas_call x1, Pallas kernels, placed_outputs(): pl.pallas_call(place_kernel, out_shape=(jax.ShapeDtypeStruct((L, C), BF16...  2.43 us

profile of v7, /device:TPU:1, one launch (start us, length us, event | category | flops | bytes accessed | tf_op | source)
XLA Modules:
  0.0 84.4 jit_solution(10769976079837248671)
XLA Ops:
  0.6 81.4 %whole.1 = (bf16[256,1536]{1,0:T(8,128)(2,1)}, f32[96,1536]{1,0:T(8,128)}, f32[8,1536]{1,0:T(8,128)}) custom-call(s32[1,256]{1,0:T(1,128)} %tok_in.1, bf16[4,1536]{1,0:T(4,128)(2,1)} %emb_in.1, f32[3,1536]{1,0:T(4,128)} %k1_in.1, f32[1536]{0:T(1024)} %g1_in.1, bf16[48,1536]{1,0:T(8,128)(2,1)} %w1_in.1, f32[3,1536]{1,0:T(4,128)} %k2_in.1, f32[1536]{0:T(1024)} %g2_in.1, ...), custom_call_target="tpu_custom_call" | custom-call | tf_op jit(solution)/shard_map/whole/pallas_call | solution.py:711
  82.0 2.4 %place.1 = (bf16[256,1536]{1,0:T(8,128)(2,1)}, f32[48,1536]{1,0:T(8,128)}, f32[48,1536]{1,0:T(8,128)}, f32[3,1536]{1,0:T(4,128)}, f32[3,1536]{1,0:T(4,128)}, /*index=5*/f32[1536]{0:T(1024)}, f32[1536]{0:T(1024)}) custom-call(bf16[256,1536]{1,0:T(8,128)(2,1)} %get-tuple-element.17.out_in, f32[96,1536]{1,0:T(8,128)} %get-tuple-element.18.gw_in, ...), custom_call_target="tpu_custom_call" | custom-call | tf_op jit(solution)/shard_map/place/pallas_call | solution.py:795
